TPU v7x, 256 devices: a whole 4x4x8 slice. The times are simulated.
256 devices in a mesh: row: 16 (over x, z_lo, core), col: 16 (over y, z_hi).
Axes of the slice: x: 4, y: 4, z: 8 (z_hi: 4, z_lo: 2; z = z_hi * 2 + z_lo), core: 2. Of those that a mesh axis runs over, the one named last changes fastest.
Arguments:
- matrix: float32 [16384, 16384], P('row', 'col'), as said below
- pivots: int32 [256], replicated, may hold values from 256 to 16383, as said below
- coupling: float32 [256, 256], replicated, as said below
Outputs:
- trailing: float32 [16384, 16384], P('row', 'col')
Inputs may be any that keep to these rules, and one draw needn't show every extreme that they name: `pivots`: 256 distinct row indices, all at or beyond 256; among them are the last row and row 8192. `matrix`: exactly symmetric. `coupling`: exactly symmetric.
All inputs are finite; a program needn't handle non-finite values.
Results may differ from a plain program's by a relative error of at most 0.000053.
Values sent between devices are 32-bit elements; how exact they have to be, the bound alone decides.
A program may use at most 64 MiB of HBM per device.

v0:
```python
import jax
import jax.numpy as jnp
from jax import lax
from jax.sharding import PartitionSpec as P


def broadcast(x, axis, root):
    mine = lax.axis_index(axis) == root
    return lax.psum(jnp.where(mine, x, jnp.zeros_like(x)), axis)


def pick_columns(block, targets, start, width):
    count = block.shape[1]
    local = targets - start
    inside = (local >= 0) & (local < count)
    picked = jnp.where(
        inside[None, :], jnp.take(block, jnp.clip(local, 0, count - 1), axis=1), jnp.float32(0.0)
    )
    leading = jnp.where(start == 0, block[:, :width], jnp.float32(0.0))
    return (leading, picked)


def place_columns(block, targets, start, width, lead_vals, pivot_vals):
    count = block.shape[1]
    local = targets - start
    inside = (local >= 0) & (local < count)
    spots = jnp.where(inside, local, count)
    done = block.at[:, spots].set(lead_vals, mode="drop")
    left = jnp.where(start == 0, pivot_vals, done[:, :width])
    return lax.dynamic_update_slice(done, left, (0, 0))


def per_device(matrix, pivots, coupling):
    rows_dev, cols_dev = matrix.shape
    width = coupling.shape[0]
    row_start = lax.axis_index("row") * rows_dev
    col_start = lax.axis_index("col") * cols_dev
    local_r = pivots - row_start
    inside_r = (local_r >= 0) & (local_r < rows_dev)
    picked = jnp.where(
        inside_r[:, None],
        jnp.take(matrix, jnp.clip(local_r, 0, rows_dev - 1), axis=0),
        jnp.float32(0.0),
    )
    leading = jnp.where(row_start == 0, matrix[:width], jnp.float32(0.0))
    lead_rows, pivot_rows = lax.psum((leading, picked), "row")
    spots_r = jnp.where(inside_r, local_r, rows_dev)
    rows_done = matrix.at[spots_r].set(lead_rows, mode="drop")
    top = jnp.where(row_start == 0, pivot_rows, rows_done[:width])
    rows_done = lax.dynamic_update_slice(rows_done, top, (0, 0))
    lead_c, picked_c = pick_columns(rows_done, pivots, col_start, width)
    lead_cols, pivot_cols = lax.psum((lead_c, picked_c), "col")
    permuted = place_columns(rows_done, pivots, col_start, width, lead_cols, pivot_cols)
    panel_top = broadcast(permuted[:width], "row", 0)
    scaled = jnp.dot(
        pivot_cols, coupling, precision=lax.Precision.HIGHEST, preferred_element_type=jnp.float32
    )
    update = jnp.dot(
        scaled, panel_top, precision=lax.Precision.HIGHEST, preferred_element_type=jnp.float32
    )
    global_rows = row_start + lax.broadcasted_iota(jnp.int32, (rows_dev, cols_dev), 0)
    global_cols = col_start + lax.broadcasted_iota(jnp.int32, (rows_dev, cols_dev), 1)
    return jnp.where(global_rows >= global_cols, permuted - update, jnp.float32(0.0))


def solution(mesh):
    return jax.shard_map(
        per_device,
        mesh=mesh,
        in_specs=(P("row", "col"), P(), P()),
        out_specs=P("row", "col"),
        check_vma=False,
    )
```

profile of v0, /device:TPU:1, one launch (start us, length us, event | category | flops | bytes accessed | tf_op | source)
XLA Modules:
  0.0 506.9 jit_solution(8284039780969157967)
XLA Ops:
  6.5 4.8 copy.26
  11.4 3.8 gather_fusion
  15.3 0.3 copy.7
  15.6 0.3 copy.15
  16.0 1.5 select_select_fusion
  17.6 133.1 %all-reduce.10.cloned.1.call-done = (f32[256,1024]{0,1:T(8,128)}, f32[256,1024]{0,1:T(8,128)}) async-done(((f32[256,1024]{0,1:T(8,128)}, f32[256,1024]{0,1:T(8,128)}), (f32[256,1024]{0,1:T(8,128)}, f32[256,1024]{0,1:T(8,128)})) %all-reduce.10.cloned.1.call-update) | async-done | bytes 2097168 | tf_op jit(solution)/shard_map/psum | solution.py:46
  150.6 1.6 copy.6
  152.2 5.6 %scatter_fusion = f32[1024,1024]{1,0:T(8,128)} fusion(f32[1024,1024]{1,0:T(8,128)} %copy.26, s32[256]{0:T(256)S(1)} %get-tuple-element.20, f32[256,1024]{1,0:T(8,128)S(1)} %copy.6), kind=kCustom, calls=%fused_computation.2 | custom fusion | bytes 3146752 | tf_op jit(solution)/shard_map/scatter | solution.py:48
  157.8 5.4 %copy.10 = f32[1024,1024]{0,1:T(8,128)} copy(f32[1024,1024]{1,0:T(8,128)} %scatter_fusion) | data formatting | bytes 8388608 | tf_op jit(solution)/shard_map/scatter | solution.py:48
  163.2 2.4 fusion
  165.6 3.8 gather_fusion.1
  169.4 0.3 copy.11
  169.8 0.3 copy.12
  170.1 2.3 slice_select_fusion.2
  172.4 1.1 select_bitcast_fusion
  173.6 172.4 %all-reduce.8.cloned.1.call-done = (f32[1024,256]{0,1:T(8,128)}, f32[1024,256]{0,1:T(8,128)}) async-done(((f32[1024,256]{0,1:T(8,128)}, f32[1024,256]{0,1:T(8,128)}), (f32[1024,256]{0,1:T(8,128)}, f32[1024,256]{0,1:T(8,128)})) %all-reduce.8.cloned.1.call-update) | async-done | bytes 2097168 | tf_op jit(solution)/shard_map/psum | solution.py:52
  346.0 6.3 %scatter_custom_fusion.1 = f32[1024,1024]{0,1:T(8,128)} fusion(f32[1024,1024]{0,1:T(8,128)} %fusion, s32[256]{0:T(256)S(1)} %get-tuple-element.19, f32[1024,256]{0,1:T(8,128)} %get-tuple-element.5), kind=kCustom, calls=%fused_computation.10 | custom fusion | bytes 5242880 | tf_op jit(solution)/shard_map/scatter | solution.py:28
  352.3 5.4 %copy.13 = f32[1024,1024]{1,0:T(8,128)} copy(f32[1024,1024]{0,1:T(8,128)} %scatter_custom_fusion.1) | data formatting | bytes 8388608 | tf_op jit(solution)/shard_map/scatter | solution.py:28
  357.7 1.4 slice_select_fusion.1
  359.4 1.0 constant_dynamic-update-slice_fusion
  360.5 2.4 slice_select_fusion
  362.9 1.8 fusion.3
  364.7 128.5 %all-reduce.6.cloned.1.call-done = f32[256,1024]{1,0:T(8,128)} async-done(((f32[256,1024]{1,0:T(8,128)}), f32[256,1024]{1,0:T(8,128)}) %all-reduce.6.cloned.1.call-update) | async-done | bytes 1048592 | tf_op jit(solution)/shard_map/psum | solution.py:9
  493.2 7.1 %subtract_select_fusion = f32[1024,1024]{1,0:T(8,128)} fusion(f32[1024,1024]{1,0:T(8,128)} %constant_dynamic-update-slice_fusion, f32[1024,256]{1,0:T(8,128)S(1)} %fusion.3, f32[256,1024]{1,0:T(8,128)} %all-reduce.6.cloned.1.call-done, s32[1024]{0:T(1024)S(1)} %get-tuple-element.23, s32[1024]{0:T(1024)S(1)} %get-tuple-element.24), kind=kOutput, calls=%fused_computation.4 | convolution fusion | flops 3224371200 | bytes 10493952 | tf_op jit(solution)/shard_map/dot_general | solution.py:58
  (23 shorter events, 0.6 us)
Async XLA Ops:
  6.5 356.3 %copy-start = (f32[256,256]{1,0:T(8,128)S(1)}, f32[256,256]{1,0:T(8,128)}, u32[]{:S(2)}) copy-start(f32[256,256]{1,0:T(8,128)} %param.5) | copy-start | bytes 786436
  6.5 4.8 copy-start.3
  6.5 144.1 %all-reduce.10.cloned.1.call-start = ((), (), s32[]{:S(2)}) async-start(), calls=%async_computation.2 | async-start | bytes 4194304 | tf_op jit(solution)/shard_map/psum | solution.py:46
  11.4 4.2 slice-start
  17.5 328.6 %all-reduce.8.cloned.1.call-start = ((), (), s32[]{:S(2)}) async-start(), calls=%async_computation.1 | async-start | bytes 4194304 | tf_op jit(solution)/shard_map/psum | solution.py:52
  157.8 5.5 %copy-start.2 = (f32[256,1024]{0,1:T(8,128)S(1)}, f32[256,1024]{0,1:T(8,128)}, u32[]{:S(2)}) copy-start(f32[256,1024]{0,1:T(8,128)} %get-tuple-element.8) | copy-start | bytes 3145732
  173.6 319.7 %all-reduce.6.cloned.1.call-start = ((), (), s32[]{:S(2)}) async-start(), calls=%async_computation | async-start | bytes 2097152 | tf_op jit(solution)/shard_map/psum | solution.py:9
  352.3 5.4 %copy-start.1 = (f32[1024,256]{0,1:T(8,128)S(1)}, f32[1024,256]{0,1:T(8,128)}, u32[]{:S(2)}) copy-start(f32[1024,256]{0,1:T(8,128)} %get-tuple-element.6) | copy-start | bytes 3145732
Sparse Core Ops, SparseCore 0:
  17.6 132.9 all-reduce.9
  173.7 172.2 all-reduce.7
  363.0 130.2 all-reduce.5
where the time goes:
time: 507 us
  waiting for transfers between devices  434 us (86%)
  local copies, waits for them, and re-layouts  39.4 us (8%)
  between operations  13.3 us (3%)
  other arithmetic  11.2 us (2%)
  matrix products  8.96 us (2%)
    psum x1, waiting for transfers between devices, per_device(): lead_cols, pivot_cols = lax.psum((lead_c, picked_c), 'col')  172 us
    psum x1, waiting for transfers between devices, per_device(): lead_rows, pivot_rows = lax.psum((leading, picked), 'row')  133 us
    psum x1, waiting for transfers between devices, broadcast(): return lax.psum(jnp.where(mine, x, jnp.zeros_like(x)), axis)  129 us
    scatter x2, local copies, waits for them, and re-layouts, place_columns(): done = block.at[:, spots].set(lead_vals, mode='drop')  11.7 us
    scatter x2, local copies, waits for them, and re-layouts, per_device(): rows_done = matrix.at[spots_r].set(lead_rows, mode='drop')  11 us
  transfers between devices with their start and end apart: 3, of which 3 were waited for; matrix products, arithmetic and copies ran while one was open for 0% of the time, Pallas kernels for 0%

commit v1 on v0

v1 whole, which is shorter than its diff:
```python
import functools

import jax
import jax.numpy as jnp
from jax import lax
from jax.experimental import pallas as pl
from jax.experimental.pallas import tpu as pltpu
from jax.sharding import PartitionSpec as P

MESH = pl.DeviceIdType.MESH
F32 = jnp.float32
BF16 = jnp.bfloat16
HIGHEST = lax.Precision.HIGHEST


def one_hot(index, start, shape, axis):
    return lax.broadcasted_iota(jnp.int32, shape, axis) + start == index


def pick_kernel(piv, matrix, picked, sem):
    rows = matrix.shape[0]
    count = picked.shape[0]
    start = lax.axis_index("row") * rows
    picked[...] = jnp.zeros_like(picked)

    def copy(k):
        local = jnp.clip(piv[k] - start, 0, rows - 1)
        return pltpu.make_async_copy(matrix.at[pl.ds(local, 1)], picked.at[pl.ds(k, 1)], sem)

    def go(k, _):
        @pl.when((piv[k] >= start) & (piv[k] < start + rows))
        def _():
            copy(k).start()

        return 0

    def wait(k, _):
        @pl.when((piv[k] >= start) & (piv[k] < start + rows))
        def _():
            copy(k).wait()

        return 0

    lax.fori_loop(0, count, go, 0)
    lax.fori_loop(0, count, wait, 0)


def pick(matrix, pivots):
    return pl.pallas_call(
        pick_kernel,
        out_shape=jax.ShapeDtypeStruct((pivots.shape[0], matrix.shape[1]), F32),
        in_specs=[pl.BlockSpec(memory_space=pltpu.SMEM), pl.BlockSpec(memory_space=pl.ANY)],
        out_specs=pl.BlockSpec(memory_space=pltpu.VMEM),
        scratch_shapes=[pltpu.SemaphoreType.DMA],
        name="pick",
    )(pivots, matrix)


def exchange_kernel(
    picked, matrix, piv_col, piv_row, qc, qr,
    a1buf, sums, a2buf, raw, piece, corner, w0buf, w0mine,
    s_a1, r_a1, s_a2, r_a2, s_ld, r_ld, s_w, r_w, s_w0, r_w0,
    s_b, r_b, s_f, s_t, r_t, s_y, r_y, local,
):
    r, c = lax.axis_index("row"), lax.axis_index("col")
    width, cols = picked.shape
    own = raw.shape[1]
    q, core = lax.div(r, 2), lax.rem(r, 2)
    x, y, zh = lax.div(r, 4), lax.div(c, 4), lax.rem(c, 4)
    sib = r + 1 - 2 * core
    col_start = c * cols

    def remote(src, dst, ssem, rsem, row, col):
        return pltpu.make_async_remote_copy(
            src_ref=src, dst_ref=dst, send_sem=ssem, recv_sem=rsem,
            device_id=(row, col), device_id_type=MESH,
        )

    def arrived(dst, rsem):
        remote(dst, dst, rsem, rsem, sib, c).wait_recv()

    def signal(row, col):
        pl.semaphore_signal(barrier, inc=1, device_id=(row, col), device_id_type=MESH)

    def slots(g, n=1):
        return pl.ds(pl.multiple_of(g * own, own), n * own)

    barrier = pltpu.get_barrier_semaphore()
    for d in range(1, 16):
        signal(lax.rem(r + d, 16), c)
    for d in range(1, 4):
        signal(r, lax.rem(y + d, 4) * 4 + zh)
    for j in range(4):
        @pl.when((r != c) | (4 * y + j != r))
        def _():
            signal(4 * y + j, r)

    @pl.when(c != 0)
    def _():
        signal(r, 0)

    @pl.when(c == 0)
    def _():
        for b in range(1, 16):
            signal(r, b)

    greeted = 15 + 3 + 4 - jnp.where(r == c, 1, 0) + jnp.where(c == 0, 15, 1)
    pl.semaphore_wait(barrier, greeted)

    def lead_copies(act):
        @pl.when(r == 0)
        def _():
            for g in range(1, 16):
                act(remote(matrix.at[slots(g)], raw.at[1], s_ld.at[g], r_ld.at[0], g, c))
            act(pltpu.make_async_copy(matrix.at[slots(0)], raw.at[1], local.at[0]))

    lead_copies(lambda copy: copy.start())

    def a1(p):
        return remote(
            picked.at[slots(2 * p + 1 - core)], a1buf.at[p], s_a1.at[p], r_a1.at[p], sib, c
        )

    def a2(p):
        return remote(sums.at[p], a2buf.at[q], s_a2.at[p], r_a2.at[q], 2 * p + core, c)

    for d in range(1, 9):
        a1(lax.rem(q + d, 8)).start()
    for d in range(1, 9):
        p = lax.rem(q + d, 8)
        arrived(a1buf.at[p], r_a1.at[p])
        total = picked[slots(2 * p + core)] + a1buf[p]
        if d < 8:
            sums[p] = total
            a2(p).start()
        else:
            a2buf[q] = total

    hot_t = one_hot(piv_col[...], col_start, (width, cols), 1).astype(F32)
    swapped = jnp.max(hot_t, axis=0, keepdims=True) > 0

    def fixed(part):
        placed = jnp.dot(corner[part], hot_t, precision=HIGHEST, preferred_element_type=F32)
        return jnp.where(swapped, placed, raw[part])

    def send_corner(part, act):
        for b in range(1, 16):
            act(remote(corner.at[part], corner.at[part], s_w.at[part, b], r_w.at[part], r, b))

    def get_corner(part):
        @pl.when(c == 0)
        def _():
            corner[part] = raw[part, :, :width]
            send_corner(part, lambda copy: copy.start())

        @pl.when(c != 0)
        def _():
            arrived(corner.at[part], r_w.at[part])

    def b_copy(part, d):
        p = lax.rem(q + d, 8)
        return p, remote(
            piece.at[part], qc.at[part, slots(r)], s_b.at[part, d], r_b.at[part, r], 2 * p + core, c
        )

    def b_copies(part, act):
        for d in range(1, 8):
            p, copy = b_copy(part, d)

            @pl.when(2 * p + 1 >= c)
            def _():
                act(copy)

    def f_copy(part, d):
        if d == 0:
            return remote(
                piece.at[part], qc.at[part, slots(r)], s_f.at[part, 0], r_b.at[part, r], sib, c
            )
        g = 2 * lax.rem(q + d, 8) + core
        return remote(
            qc.at[part, slots(g)], qc.at[part, slots(g)], s_f.at[part, d], r_b.at[part, g], sib, c
        )

    def t_copies(part, act):
        for k in range(4):
            col = 4 * x + k
            here = (r == c) & (k == zh)

            @pl.when(jnp.logical_not(here))
            def _():
                act(
                    remote(
                        piece.at[part], qr.at[part, slots(r)],
                        s_t.at[part, k], r_t.at[part, lax.rem(r, 4)], c, col,
                    )
                )

            @pl.when(here)
            def _():
                act(
                    pltpu.make_async_copy(
                        piece.at[part], qr.at[part, slots(r)], local.at[3 + part]
                    )
                )

    def send_piece(part):
        b_copies(part, lambda copy: copy.start())
        t_copies(part, lambda copy: copy.start())

        @pl.when(sib >= c)
        def _():
            f_copy(part, 0).start()

        pltpu.make_async_copy(piece.at[part], qc.at[part, slots(r)], local.at[1 + part]).start()

    @pl.when(r == 0)
    def _():
        pltpu.make_async_copy(matrix.at[slots(0)], raw.at[1], local.at[0]).wait()

    @pl.when(r != 0)
    def _():
        arrived(raw.at[1], r_ld.at[0])

    get_corner(1)
    piece[1] = fixed(1)
    send_piece(1)

    for d in range(1, 8):
        p = lax.rem(q + d, 8)
        arrived(a2buf.at[p], r_a2.at[p])
    total = a2buf[0]
    for p in range(1, 8):
        total = total + a2buf[p]
    raw[0] = total
    get_corner(0)
    hot = one_hot(piv_row[...], col_start, (cols, width), 0).astype(F32)
    mine = jnp.dot(total, hot, precision=HIGHEST, preferred_element_type=F32)

    def w0_copy(col):
        return remote(w0mine, w0buf.at[col], s_w0.at[0], r_w0.at[col], r, 0)

    @pl.when(c != 0)
    def _():
        w0mine[...] = mine
        w0_copy(c).start()

    piece[0] = fixed(0)

    @pl.when(c == 0)
    def _():
        w0 = mine
        for b in range(1, 16):
            arrived(w0buf.at[b], r_w0.at[b])
            w0 = w0 + w0buf[b]
        piece[0, :, :width] = w0

    send_piece(0)

    def y_copies(part, act):
        for d in range(1, 4):
            col = lax.rem(y + d, 4) * 4 + zh

            @pl.when(col <= r)
            def _():
                block = qr.at[part, slots(4 * y, 4)]
                act(remote(block, block, s_y.at[part, d], r_y.at[part, y], r, col))

    def run_y(part):
        for j in range(4):
            here = (r == c) & (4 * y + j == r)

            @pl.when(jnp.logical_not(here))
            def _():
                arrived(qr.at[part, slots(4 * y + j)], r_t.at[part, j])

            @pl.when(here)
            def _():
                pltpu.make_async_copy(
                    piece.at[part], qr.at[part, slots(r)], local.at[3 + part]
                ).wait()

        y_copies(part, lambda copy: copy.start())

    def run_f(part):
        for d in range(1, 8):
            g = 2 * lax.rem(q + d, 8) + core

            @pl.when(2 * q + 1 >= c)
            def _():
                arrived(qc.at[part, slots(g)], r_b.at[part, g])

            @pl.when(sib >= c)
            def _():
                f_copy(part, d).start()

    run_y(1)
    run_y(0)
    run_f(1)
    run_f(0)

    for part in (1, 0):
        for d in range(8):
            g = 2 * lax.rem(q + d, 8) + 1 - core

            @pl.when(r >= c)
            def _():
                arrived(qc.at[part, slots(g)], r_b.at[part, g])

        for d in range(1, 4):
            there = lax.rem(y + d, 4)

            @pl.when(c <= r)
            def _():
                arrived(qr.at[part, slots(4 * there, 4)], r_y.at[part, there])

        pltpu.make_async_copy(piece.at[part], qc.at[part, slots(r)], local.at[1 + part]).wait()

    lead_copies(lambda copy: copy.wait_send() if copy.is_remote else None)
    for d in range(1, 9):
        a1(lax.rem(q + d, 8)).wait_send()
    for d in range(1, 8):
        a2(lax.rem(q + d, 8)).wait_send()

    @pl.when(c != 0)
    def _():
        w0_copy(c).wait_send()

    for part in (1, 0):
        @pl.when(c == 0)
        def _():
            send_corner(part, lambda copy: copy.wait_send())

        b_copies(part, lambda copy: copy.wait_send())
        t_copies(part, lambda copy: copy.wait_send() if copy.is_remote else None)
        y_copies(part, lambda copy: copy.wait_send())

        @pl.when(sib >= c)
        def _():
            for d in range(8):
                f_copy(part, d).wait_send()


def exchange(picked, matrix, piv_col, piv_row):
    width, cols = picked.shape
    own = width // 16
    dma = pltpu.SemaphoreType.DMA
    out = jax.ShapeDtypeStruct((2, width, cols), F32)
    any_spec = pl.BlockSpec(memory_space=pl.ANY)
    vmem = pl.BlockSpec(memory_space=pltpu.VMEM)
    return pl.pallas_call(
        exchange_kernel,
        out_shape=(out, out),
        in_specs=[vmem, any_spec, vmem, vmem],
        out_specs=(any_spec, any_spec),
        scratch_shapes=[
            pltpu.VMEM((8, own, cols), F32),
            pltpu.VMEM((8, own, cols), F32),
            pltpu.VMEM((8, own, cols), F32),
            pltpu.VMEM((2, own, cols), F32),
            pltpu.VMEM((2, own, cols), F32),
            pltpu.VMEM((2, own, width), F32),
            pltpu.VMEM((16, own, width), F32),
            pltpu.VMEM((own, width), F32),
            dma((8,)), dma((8,)), dma((8,)), dma((8,)),
            dma((16,)), dma((1,)), dma((2, 16)), dma((2,)), dma((1,)), dma((16,)),
            dma((2, 8)), dma((2, 16)), dma((2, 8)), dma((2, 4)), dma((2, 4)), dma((2, 4)), dma((2, 4)),
            dma((5,)),
        ],
        compiler_params=pltpu.CompilerParams(
            collective_id=0, has_side_effects=True, vmem_limit_bytes=32 * 1024 * 1024
        ),
        name="exchange",
    )(picked, matrix, piv_col, piv_row)


def split(value, n):
    terms = []
    for _ in range(n):
        term = value.astype(BF16)
        terms.append(term)
        value = value - term.astype(F32)
    return terms


def update_kernel(piv_col, piv_row, m, qc, qr, coupling, out, hot_t, panel, lead):
    r, c = lax.axis_index("row"), lax.axis_index("col")
    tile, cols = out.shape
    width = coupling.shape[0]
    step = pl.program_id(0)
    row_start = r * cols + step * tile
    col_start = c * cols

    @pl.when(r < c)
    def _():
        out[...] = jnp.zeros_like(out)

    @pl.when((r >= c) & (step == 0))
    def _():
        hot_t[...] = one_hot(piv_col[...], col_start, (width, cols), 1).astype(BF16)
        for i, term in enumerate(split(qc[0], 2)):
            panel[i] = term
        for i, term in enumerate(split(qc[1], 3)):
            lead[i] = term

    def dot(a, b):
        return jnp.dot(a, b, preferred_element_type=F32)

    @pl.when(r >= c)
    def _():
        panel_rows = qr[0].T
        scaled = jnp.dot(panel_rows, coupling[...], precision=HIGHEST, preferred_element_type=F32)
        s_hi, s_lo = split(scaled, 2)
        update = dot(s_hi, panel[0]) + dot(s_hi, panel[1]) + dot(s_lo, panel[0])
        hot = one_hot(piv_row[...], row_start, (tile, width), 0)
        hit_row = jnp.max(hot.astype(F32), axis=1, keepdims=True) > 0
        hit_col = jnp.max(hot_t[...].astype(F32), axis=0, keepdims=True) > 0
        hot = hot.astype(F32).astype(BF16)
        new_rows = dot(hot, lead[0]) + dot(hot, lead[1]) + dot(hot, lead[2])
        lead_cols = jnp.where(hit_row, 0.0, qr[1].T)
        new_cols = sum(dot(term, hot_t[...]) for term in split(lead_cols, 3))
        value = jnp.where(hit_row | hit_col, 0.0, m[...]) + new_rows + new_cols
        spread = jnp.concatenate([panel_rows, jnp.zeros((tile, cols - width), F32)], axis=1)
        places = lax.broadcasted_iota(jnp.int32, (tile, cols), 1)
        value = jnp.where((places < width) & (c == 0), spread, value)
        below = lax.broadcasted_iota(jnp.int32, (tile, cols), 0) + row_start >= places + col_start
        out[...] = jnp.where(below, value - update, 0.0)


def update(piv_col, piv_row, matrix, qc, qr, coupling):
    rows, cols = matrix.shape
    width = coupling.shape[0]
    tile = min(rows, 256)

    def whole(shape):
        return pl.BlockSpec(shape, lambda i: (0,) * len(shape))

    return pl.pallas_call(
        update_kernel,
        grid=(rows // tile,),
        out_shape=jax.ShapeDtypeStruct((rows, cols), F32),
        in_specs=[
            whole((width, 1)),
            whole((1, width)),
            pl.BlockSpec((tile, cols), lambda i: (i, 0)),
            whole((2, width, cols)),
            pl.BlockSpec((2, width, tile), lambda i: (0, 0, i)),
            whole((width, width)),
        ],
        out_specs=pl.BlockSpec((tile, cols), lambda i: (i, 0)),
        scratch_shapes=[
            pltpu.VMEM((width, cols), BF16),
            pltpu.VMEM((2, width, cols), BF16),
            pltpu.VMEM((3, width, cols), BF16),
        ],
        compiler_params=pltpu.CompilerParams(vmem_limit_bytes=48 * 1024 * 1024),
        name="update",
    )(piv_col, piv_row, matrix, qc, qr, coupling)


def per_device(matrix, pivots, coupling):
    width = coupling.shape[0]
    piv_col, piv_row = pivots.reshape(width, 1), pivots.reshape(1, width)
    picked = pick(matrix, pivots)
    qc, qr = exchange(picked, matrix, piv_col, piv_row)
    return update(piv_col, piv_row, matrix, qc, qr, coupling)


def solution(mesh):
    return jax.shard_map(
        per_device,
        mesh=mesh,
        in_specs=(P("row", "col"), P(), P()),
        out_specs=P("row", "col"),
        check_vma=False,
    )
```

time: 507 us -> 99.6 us (0.20)
  the two profiles are of different devices: /device:TPU:1 before, /device:TPU:54 now
where the time goes in v1:
time: 99.6 us; the launch traced here: 99.3 us
  Pallas kernels  94.9 us (95%)
  local copies, waits for them, and re-layouts  4.29 us (4%)
    pallas_call x1, Pallas kernels, exchange(): pl.pallas_call(exchange_kernel, out_shape=(out, out), in_specs=[vmem, any...  75.4 us
    pallas_call x1, Pallas kernels, update(): pl.pallas_call(update_kernel, grid=(rows // tile,), out_shape=jax.ShapeDt...  10.9 us
    pallas_call x1, Pallas kernels, pick(): pl.pallas_call(pick_kernel, out_shape=jax.ShapeDtypeStruct((pivots.shape[...  8.6 us
    unnamed x8, local copies, waits for them, and re-layouts  3.42 us

profile of v1, /device:TPU:54, one launch (start us, length us, event | category | flops | bytes accessed | tf_op | source)
XLA Modules:
  0.0 99.3 jit_solution(11769206786754202802)
XLA Ops:
  0.0 0.0 copy-start.3
  0.0 0.9 copy.5.piv_col
  0.9 0.0 copy-start.2
  0.9 8.6 %pick.1.picked = f32[256,1024]{1,0:T(8,128)} custom-call(s32[256]{0:T(256)} %piv.1, f32[1024,1024]{1,0:T(8,128)} %m.1), custom_call_target="tpu_custom_call" | custom-call | tf_op jit(solution)/shard_map/pick/pallas_call | solution.py:49
  9.5 0.0 copy-done.3
  9.5 0.0 copy-start
  9.5 2.2 %copy-done = f32[1024,1024]{1,0:T(8,128)S(1)} copy-done((f32[1024,1024]{1,0:T(8,128)S(1)}, f32[1024,1024]{1,0:T(8,128)}, u32[]{:S(2)}) %copy-start) | copy-done | bytes 4194328
  11.7 0.0 copy-start.1
  11.7 1.2 %copy-done.1 = f32[256,1024]{1,0:T(8,128)S(1)} copy-done((f32[256,1024]{1,0:T(8,128)S(1)}, f32[256,1024]{1,0:T(8,128)}, u32[]{:S(2)}) %copy-start.1) | copy-done | bytes 1048600
  12.9 75.4 %exchange.1 = (f32[2,256,1024]{2,1,0:T(8,128)S(1)}, f32[2,256,1024]{2,1,0:T(8,128)S(1)}) custom-call(f32[256,1024]{1,0:T(8,128)S(1)} %copy-done.1, f32[1024,1024]{1,0:T(8,128)S(1)} %copy-done, s32[256,1]{1,0:T(8,128)S(1)} %copy.5.piv_col, s32[1,256]{1,0:T(1,128)S(1)} %bitcast.3), custom_call_target="tpu_custom_call" | custom-call | tf_op jit(solution)/shard_map/exchange/pallas_call | solution.py:350
  88.3 0.0 copy-done.2
  88.3 10.9 %update.1 = f32[1024,1024]{1,0:T(8,128)} custom-call(s32[256,1]{1,0:T(8,128)S(1)} %copy.5.piv_col, s32[1,256]{1,0:T(1,128)S(1)} %bitcast.4, f32[1024,1024]{1,0:T(8,128)} %m.1, f32[2,256,1024]{2,1,0:T(8,128)S(1)} %get-tuple-element.7.qc, f32[2,256,1024]{2,1,0:T(8,128)S(1)} %get-tuple-element.8.qr, f32[256,256]{1,0:T(8,128)S(1)} %copy-done.2), custom_call_target="tpu_custom_call" | custom-call | tf_op jit(solution)/shard_map/update/pallas_call | solution.py:437
Async XLA Ops:
  0.0 9.5 %copy-start.3 = (s32[256]{0:T(256)S(1)}, s32[256]{0:T(256)}, u32[]{:S(2)}) copy-start(s32[256]{0:T(256)} %piv.1) | copy-start | bytes 3076
  0.9 87.4 %copy-start.2 = (f32[256,256]{1,0:T(8,128)S(1)}, f32[256,256]{1,0:T(8,128)}, u32[]{:S(2)}) copy-start(f32[256,256]{1,0:T(8,128)} %coupling.1) | copy-start | bytes 786436
  9.5 2.2 %copy-start = (f32[1024,1024]{1,0:T(8,128)S(1)}, f32[1024,1024]{1,0:T(8,128)}, u32[]{:S(2)}) copy-start(f32[1024,1024]{1,0:T(8,128)} %m.1) | copy-start | bytes 12582916
  11.7 1.2 %copy-start.1 = (f32[256,1024]{1,0:T(8,128)S(1)}, f32[256,1024]{1,0:T(8,128)}, u32[]{:S(2)}) copy-start(f32[256,1024]{1,0:T(8,128)} %pick.1.picked) | copy-start | bytes 3145732

commit v2 on v1

--- a/solution.py
+++ b/solution.py
@@ -11,6 +11,7 @@
 F32 = jnp.float32
 BF16 = jnp.bfloat16
 HIGHEST = lax.Precision.HIGHEST
+CAP = 32
 
 
 def one_hot(index, start, shape, axis):
@@ -457,12 +458,580 @@
     )(piv_col, piv_row, matrix, qc, qr, coupling)
 
 
+def order(s):
+    return lax.rem(s, 2) * 8 + lax.div(s, 2)
+
+
+def blocks_of(piv, rows):
+    block = jnp.right_shift(piv, rows.bit_length() - 1)
+    return jnp.bitwise_and(block, 1) * 8 + jnp.right_shift(block, 1)
+
+
+def places(piv_col, piv_row, rows):
+    width = piv_col.shape[0]
+    first = lax.broadcasted_iota(jnp.int32, (width, width), 0)
+    second = lax.broadcasted_iota(jnp.int32, (width, width), 1)
+    block_col, block_row = blocks_of(piv_col, rows), blocks_of(piv_row, rows)
+    same = block_col == block_row
+    rank_col = jnp.sum(jnp.where(same & (second < first), 1, 0), axis=1, keepdims=True)
+    rank_row = jnp.sum(jnp.where(same & (first < second), 1, 0), axis=0, keepdims=True)
+    return block_col * CAP + rank_col, block_row * CAP + rank_row
+
+
+def listed(place_row, piv_row, start, count):
+    spot = lax.broadcasted_iota(jnp.int32, (count, place_row.shape[1]), 0) + start
+    return jnp.sum(jnp.where(spot == place_row, piv_row + 1, 0), axis=1, keepdims=True) - 1
+
+
+def compact_kernel(
+    matrix, piv_col, piv_row, qc, qr, swaps, corner,
+    block, picked, fixed, hall, abuf, lead, piece, kout, kin, w0out, w0in, lout,
+    s_a, r_a, s_sib, r_sib, s_ld, r_ld, s_k, r_k, s_w0, r_w0, s_l, r_l,
+    s_b, r_b, s_f, s_t, r_t, s_y, s_z, r_y, local,
+):
+    r, c = lax.axis_index("row"), lax.axis_index("col")
+    rows, cols = matrix.shape
+    width = piv_col.shape[0]
+    half, part = width // 2, cols // 8
+    q, core = lax.div(r, 2), lax.rem(r, 2)
+    x, y, zh = lax.div(r, 4), lax.div(c, 4), lax.rem(c, 4)
+    sib = r + 1 - 2 * core
+    chunk = lax.div(order(c), 4)
+
+    def remote(src, dst, ssem, rsem, row, col):
+        return pltpu.make_async_remote_copy(
+            src_ref=src, dst_ref=dst, send_sem=ssem, recv_sem=rsem,
+            device_id=(row, col), device_id_type=MESH,
+        )
+
+    def arrived(dst, rsem):
+        remote(dst, dst, rsem, rsem, sib, c).wait_recv()
+
+    def start(copy):
+        copy.start()
+
+    def sent(copy):
+        copy.wait_send()
+
+    def dot(a, b):
+        return jnp.dot(a, b, precision=HIGHEST, preferred_element_type=F32)
+
+    load = pltpu.make_async_copy(matrix, block, local.at[0])
+    load.start()
+
+    barrier = pltpu.get_barrier_semaphore()
+
+    def signal(row, col):
+        pl.semaphore_signal(barrier, inc=1, device_id=(row, col), device_id_type=MESH)
+
+    for d in range(1, 16):
+        signal(lax.rem(r + d, 16), c)
+    for d in (1, 3):
+        signal(r, lax.rem(y + d, 4) * 4 + zh)
+    for j in range(4):
+        @pl.when((r != c) | (4 * y + j != r))
+        def _():
+            signal(4 * y + j, r)
+
+    @pl.when(c != 0)
+    def _():
+        signal(r, 0)
+
+    @pl.when(c == 0)
+    def _():
+        for b in range(1, 16):
+            signal(r, b)
+
+    @pl.when(r > c)
+    def _():
+        for j in range(8):
+            signal(2 * j + lax.rem(c, 2), r)
+
+    greeted = 15 + 2 + 4 - jnp.where(r == c, 1, 0) + jnp.where(c == 0, 15, 1)
+    greeted = greeted + lax.div(c - core + 1, 2)
+
+    place_col, place_row = places(piv_col[...], piv_row[...], rows)
+    spots = lax.broadcasted_iota(jnp.int32, (16 * CAP, width), 0)
+    hall[...] = (spots == place_row).astype(F32)
+    mine = order(r) * CAP
+    have = listed(place_row, piv_row[...], mine, CAP) >= 0
+    load.wait()
+    for t in range(CAP):
+        local_row = jnp.sum(jnp.where(place_row == mine + t, piv_row[...] - r * rows, 0))
+        picked[pl.ds(t, 1)] = block[pl.ds(jnp.clip(local_row, 0, rows - 1), 1)]
+    picked[...] = jnp.where(have, picked[...], 0.0)
+
+    pl.semaphore_wait(barrier, greeted)
+
+    def lead_copy(p):
+        return remote(
+            block.at[pl.ds(0, width), pl.ds(p * part, part)], lead, s_ld.at[p], r_ld.at[0], 2 * p, c
+        )
+
+    @pl.when(r == 0)
+    def _():
+        for p in range(1, 8):
+            lead_copy(p).start()
+
+    here_piv = listed(place_row, piv_row[...], chunk * 128, 128)
+    spread = one_hot(here_piv, c * cols, (128, cols), 1).astype(F32)
+    swapped = jnp.max(spread, axis=0, keepdims=True) > 0
+
+    def k_copy(i, b):
+        return remote(
+            kout.at[i, lax.div(order(b), 4)], kin.at[i], s_k.at[i, b], r_k.at[i], r, b
+        )
+
+    def k_copies(i, act):
+        for b in range(1, 16):
+            act(k_copy(i, b))
+
+    def k_lists(i, value):
+        compact = lax.dot_general(
+            value, hall[...], (((1,), (1,)), ((), ())),
+            precision=HIGHEST, preferred_element_type=F32,
+        )
+        for j in range(4):
+            kout[i, j] = compact[:, 128 * j : 128 * (j + 1)]
+
+    def w0_copy(b):
+        return remote(w0out, w0in.at[b], s_w0.at[0], r_w0.at[b], r, 0)
+
+    @pl.when(c == 0)
+    def _():
+        k_lists(0, picked[:, :width])
+        k_copies(0, start)
+        kin[0] = kout[0, 0]
+
+    w0out[...] = lax.dot_general(
+        picked[...], spread, (((1,), (1,)), ((), ())),
+        precision=HIGHEST, preferred_element_type=F32,
+    )
+
+    @pl.when(c != 0)
+    def _():
+        w0_copy(c).start()
+        arrived(kin.at[0], r_k.at[0])
+
+    fixed[...] = jnp.where(swapped, dot(kin[0], spread), picked[...])
+
+    @pl.when(c == 0)
+    def _():
+        for b in range(1, 16):
+            arrived(w0in.at[b], r_w0.at[b])
+        w0in[0] = w0out[...]
+        total = jnp.zeros((CAP, width), F32)
+        for j in range(4):
+            listing = sum(
+                w0in[b] for b in range(16) if ((b % 2) * 8 + b // 2) // 4 == j
+            )
+            total = total + dot(listing, hall[128 * j : 128 * (j + 1)])
+        fixed[:, :width] = total
+
+    def a_copy(d):
+        p = lax.rem(q + d, 8)
+        cut = pl.ds(pl.multiple_of(p * part, part), part)
+        return remote(fixed.at[:, cut], abuf.at[core, q], s_a.at[d], r_a.at[q], 2 * p + core, c)
+
+    for d in range(1, 8):
+        a_copy(d).start()
+    abuf[core, q] = fixed[:, pl.ds(pl.multiple_of(q * part, part), part)]
+
+    lead_sib = remote(lead, lead, s_sib.at[0], r_sib.at[0], sib, c)
+
+    @pl.when(r == 0)
+    def _():
+        lead[...] = block[:width, :part]
+
+    @pl.when((core == 0) & (r != 0))
+    def _():
+        arrived(lead, r_ld.at[0])
+
+    @pl.when(core == 0)
+    def _():
+        lead_sib.start()
+
+    for d in range(1, 8):
+        p = lax.rem(q + d, 8)
+        arrived(abuf.at[core, p], r_a.at[p])
+    a_sib = remote(abuf.at[core], abuf.at[core], s_sib.at[1], r_sib.at[1], sib, c)
+    a_sib.start()
+    arrived(abuf.at[1 - core], r_sib.at[1])
+
+    lay = jnp.where(core == 0, hall[:, :half], hall[:, half:])
+    piece[...] = lax.dot_general(
+        lay, abuf[...].reshape(16 * CAP, part), (((0,), (0,)), ((), ())),
+        precision=HIGHEST, preferred_element_type=F32,
+    )
+
+    def slot(k):
+        return pl.ds(pl.multiple_of(k * half, half), half)
+
+    def t_copies(act, act_here):
+        for k in range(4):
+            here = (r == c) & (k == zh)
+
+            @pl.when(jnp.logical_not(here))
+            def _():
+                act(
+                    remote(
+                        piece, qr.at[q, slot(core)], s_t.at[k], r_t.at[lax.rem(r, 4)], c, 4 * x + k
+                    )
+                )
+
+            @pl.when(here)
+            def _():
+                act_here(pltpu.make_async_copy(piece, qr.at[q, slot(core)], local.at[1]))
+
+    def b_copies(act):
+        for d in range(1, 8):
+            p = lax.rem(q + d, 8)
+
+            @pl.when(2 * p + 1 >= c)
+            def _():
+                act(remote(piece, qc.at[q, slot(core)], s_b.at[d], r_b.at[core, q], 2 * p + core, c))
+
+    def f_copy(d):
+        p = lax.rem(q + d, 8)
+        src = piece if d == 0 else qc.at[p, slot(core)]
+        return remote(src, qc.at[p, slot(core)], s_f.at[d], r_b.at[core, p], sib, c)
+
+    t_copies(start, start)
+
+    @pl.when(sib >= c)
+    def _():
+        f_copy(0).start()
+
+    b_copies(start)
+    keep = pltpu.make_async_copy(piece, qc.at[q, slot(core)], local.at[2])
+    keep.start()
+
+    @pl.when(core == 1)
+    def _():
+        arrived(lead, r_sib.at[0])
+
+    lists = hall[pl.ds(pl.multiple_of(core * 8 * CAP, 8 * CAP), 8 * CAP)]
+    lout[...] = dot(lists, lead[...]).reshape(8, CAP, part)
+
+    def l_copies(act, act_here):
+        for j in range(8):
+            s = 2 * j + core
+            as_row = s >= c
+            row, col = jnp.where(as_row, s, c), jnp.where(as_row, c, s)
+            dst = swaps.at[jnp.where(as_row, 0, 1), q]
+            here = as_row & (s == r)
+
+            @pl.when(jnp.logical_not(here))
+            def _():
+                act(
+                    remote(lout.at[j], dst, s_l.at[j], r_l.at[jnp.where(as_row, 0, 1), q], row, col)
+                )
+
+            @pl.when(here)
+            def _():
+                act_here(j)
+
+    def keep_lead(j):
+        swaps[0, q] = lout[j]
+
+    l_copies(start, keep_lead)
+
+    def need(there):
+        return 4 * there + zh <= r
+
+    up, down, across = lax.rem(y + 1, 4), lax.rem(y + 3, 4), lax.rem(y + 2, 4)
+
+    def y_ref(owner, j):
+        return qr.at[2 * owner + j // 2, slot(j % 2)]
+
+    def y_copy(j, way):
+        col = (up if way == 0 else down) * 4 + zh
+        return remote(y_ref(y, j), y_ref(y, j), s_y.at[way, j], r_y.at[y, j], r, col)
+
+    def z_copy(j):
+        owner, to = (down, up) if j < 2 else (up, down)
+        return remote(y_ref(owner, j), y_ref(owner, j), s_z.at[j], r_y.at[owner, j], r, 4 * to + zh)
+
+    def y_copies(j, act):
+        on_up = need(up) | need(across) if j < 2 else need(up)
+        on_down = need(down) | need(across) if j >= 2 else need(down)
+
+        @pl.when(on_up)
+        def _():
+            act(y_copy(j, 0))
+
+        @pl.when(on_down)
+        def _():
+            act(y_copy(j, 1))
+
+    def z_copies(j, act):
+        @pl.when(need(up) if j < 2 else need(down))
+        def _():
+            act(z_copy(j))
+
+    for j in range(4):
+        here = (r == c) & (4 * y + j == r)
+
+        @pl.when(jnp.logical_not(here))
+        def _():
+            arrived(y_ref(y, j), r_t.at[j])
+
+        @pl.when(here)
+        def _():
+            pltpu.make_async_copy(piece, qr.at[q, slot(core)], local.at[1]).wait()
+
+        y_copies(j, start)
+
+    @pl.when((r >= c))
+    def _():
+        for p in range(8):
+            @pl.when(p != q)
+            def _():
+                arrived(swaps.at[0, p], r_l.at[0, p])
+
+    @pl.when(c == 0)
+    def _():
+        k_lists(1, jnp.concatenate([swaps[0, p] for p in range(width // part)], axis=1))
+        k_copies(1, start)
+        kin[1] = kout[1, 0]
+
+    for j in (0, 1, 2, 3):
+        owner = down if j < 2 else up
+
+        @pl.when(need(y) | (need(up) if j < 2 else need(down)))
+        def _():
+            arrived(y_ref(owner, j), r_y.at[owner, j])
+
+        z_copies(j, start)
+
+    for d in range(1, 8):
+        p = lax.rem(q + d, 8)
+
+        @pl.when(2 * q + 1 >= c)
+        def _():
+            arrived(qc.at[p, slot(core)], r_b.at[core, p])
+
+        @pl.when(sib >= c)
+        def _():
+            f_copy(d).start()
+
+    @pl.when(r >= c)
+    def _():
+        for p in range(8):
+            arrived(qc.at[p, slot(1 - core)], r_b.at[1 - core, p])
+        for j in range(4):
+            owner = up if j < 2 else down
+            arrived(y_ref(owner, j), r_y.at[owner, j])
+            arrived(y_ref(across, j), r_y.at[across, j])
+
+    @pl.when(r > c)
+    def _():
+        for p in range(8):
+            arrived(swaps.at[1, p], r_l.at[1, p])
+
+    @pl.when(c != 0)
+    def _():
+        arrived(kin.at[1], r_k.at[1])
+        w0_copy(c).wait_send()
+
+    corner[...] = kin[1]
+    keep.wait()
+
+    @pl.when(r == 0)
+    def _():
+        for p in range(1, 8):
+            lead_copy(p).wait_send()
+
+    @pl.when(core == 0)
+    def _():
+        lead_sib.wait_send()
+
+    a_sib.wait_send()
+    for d in range(1, 8):
+        a_copy(d).wait_send()
+
+    @pl.when(c == 0)
+    def _():
+        k_copies(0, sent)
+        k_copies(1, sent)
+
+    t_copies(sent, lambda copy: None)
+    b_copies(sent)
+    l_copies(sent, lambda j: None)
+    for j in range(4):
+        y_copies(j, sent)
+        z_copies(j, sent)
+
+    @pl.when(sib >= c)
+    def _():
+        for d in range(8):
+            f_copy(d).wait_send()
+
+
+def compact_exchange(matrix, piv_col, piv_row):
+    rows, cols = matrix.shape
+    width = piv_col.shape[0]
+    half, part = width // 2, cols // 8
+    dma = pltpu.SemaphoreType.DMA
+    any_spec = pl.BlockSpec(memory_space=pl.ANY)
+    vmem = pl.BlockSpec(memory_space=pltpu.VMEM)
+    panel = jax.ShapeDtypeStruct((8, width, part), F32)
+    return pl.pallas_call(
+        compact_kernel,
+        out_shape=(
+            panel,
+            panel,
+            jax.ShapeDtypeStruct((2, 8, CAP, part), F32),
+            jax.ShapeDtypeStruct((CAP, 128), F32),
+        ),
+        in_specs=[any_spec, vmem, vmem],
+        out_specs=(any_spec, any_spec, vmem, vmem),
+        scratch_shapes=[
+            pltpu.VMEM((rows, cols), F32),
+            pltpu.VMEM((CAP, cols), F32),
+            pltpu.VMEM((CAP, cols), F32),
+            pltpu.VMEM((16 * CAP, width), F32),
+            pltpu.VMEM((2, 8, CAP, part), F32),
+            pltpu.VMEM((width, part), F32),
+            pltpu.VMEM((half, part), F32),
+            pltpu.VMEM((2, 4, CAP, 128), F32),
+            pltpu.VMEM((2, CAP, 128), F32),
+            pltpu.VMEM((CAP, 128), F32),
+            pltpu.VMEM((16, CAP, 128), F32),
+            pltpu.VMEM((8, CAP, part), F32),
+            dma((8,)), dma((8,)), dma((2,)), dma((2,)), dma((8,)), dma((1,)),
+            dma((2, 16)), dma((2,)), dma((1,)), dma((16,)), dma((8,)), dma((2, 8)),
+            dma((8,)), dma((2, 8)), dma((8,)), dma((4,)), dma((4,)), dma((2, 4)), dma((4,)), dma((4, 4)),
+            dma((3,)),
+        ],
+        compiler_params=pltpu.CompilerParams(
+            collective_id=1, has_side_effects=True, vmem_limit_bytes=32 * 1024 * 1024
+        ),
+        name="compact_exchange",
+    )(matrix, piv_col, piv_row)
+
+
+def compact_update_kernel(
+    piv_col, piv_row, m, qc, qr, swaps, corner, coupling, out, panel, right, left
+):
+    r, c = lax.axis_index("row"), lax.axis_index("col")
+    tile, cols = out.shape
+    rows = tile * pl.num_programs(0)
+    width = coupling.shape[0]
+    part = qc.shape[2]
+    step = pl.program_id(0)
+    row_start = r * rows + step * tile
+    col_start = c * cols
+
+    def dot(a, b):
+        return lax.dot_general(a, b, (((0,), (0,)), ((), ())), preferred_element_type=F32)
+
+    @pl.when(r < c)
+    def _():
+        out[...] = jnp.zeros_like(out)
+
+    @pl.when((r >= c) & (step == 0))
+    def _():
+        _, place_row = places(piv_col[...], piv_row[...], rows)
+        for i in range(8):
+            for j, term in enumerate(split(qc[i], 2)):
+                panel[j, :, i * part : (i + 1) * part] = term
+        here_piv = listed(place_row, piv_row[...], lax.div(order(c), 4) * 128, 128)
+        spread = one_hot(here_piv, col_start, (128, cols), 1).astype(F32)
+        swapped = jnp.max(spread, axis=0, keepdims=True) > 0
+        lead = jnp.concatenate([swaps[0, i] for i in range(8)], axis=1)
+        placed = jnp.dot(corner[...], spread, precision=HIGHEST, preferred_element_type=F32)
+        lead = jnp.where(swapped, placed, lead)
+        for j, term in enumerate(split(lead, 3)):
+            right[j * CAP : (j + 1) * CAP] = term
+        col_piv = listed(place_row, piv_row[...], order(c) * CAP, CAP)
+        hot = one_hot(col_piv, col_start, (CAP, cols), 1).astype(F32).astype(BF16)
+        for j in range(3):
+            right[(3 + j) * CAP : (4 + j) * CAP] = hot
+        left[...] = listed(place_row, piv_row[...], order(r) * CAP, CAP)
+
+    @pl.when(r >= c)
+    def _():
+        rows_t = jnp.concatenate([qr[0], qr[1]], axis=1)
+        scaled = lax.dot_general(
+            coupling[...], rows_t, (((0,), (0,)), ((), ())),
+            precision=HIGHEST, preferred_element_type=F32,
+        )
+        s_hi, s_lo = split(scaled, 2)
+        change = dot(s_hi, panel[0]) + dot(s_hi, panel[1]) + dot(s_lo, panel[0])
+        hot = one_hot(left[...], row_start, (CAP, tile), 1).astype(F32)
+        hit = jnp.max(hot, axis=0, keepdims=True)
+        which = jnp.where(r == c, 0, 1)
+        lead = jnp.concatenate([swaps[which, 2 * step + i] for i in range(2)], axis=1)
+        lead = jnp.where(hit > 0, 0.0, lead)
+        hot = hot.astype(BF16)
+        lhs = jnp.concatenate([hot, hot, hot] + split(lead, 3), axis=0)
+        moved = dot(lhs, right[...])
+        hit_row = jnp.broadcast_to(hit, (8, tile)).T[:, :1] > 0
+        hit_col = jnp.max(right[3 * CAP : 4 * CAP].astype(F32), axis=0, keepdims=True) > 0
+        value = jnp.where(hit_row | hit_col, 0.0, m[...]) + moved
+        places_col = lax.broadcasted_iota(jnp.int32, (tile, cols), 1) + col_start
+        below = lax.broadcasted_iota(jnp.int32, (tile, cols), 0) + row_start >= places_col
+        out[...] = jnp.where(below, value - change, 0.0)
+
+        @pl.when(c == 0)
+        def _():
+            out[:, :width] = jnp.where(
+                below[:, :width], rows_t.T - change[:, :width], 0.0
+            )
+
+
+def compact_update(piv_col, piv_row, matrix, qc, qr, swaps, corner, coupling):
+    rows, cols = matrix.shape
+    width = coupling.shape[0]
+    part = cols // 8
+    tile = 2 * part
+
+    def whole(shape):
+        return pl.BlockSpec(shape, lambda i: (0,) * len(shape))
+
+    return pl.pallas_call(
+        compact_update_kernel,
+        grid=(rows // tile,),
+        out_shape=jax.ShapeDtypeStruct((rows, cols), F32),
+        in_specs=[
+            whole((width, 1)),
+            whole((1, width)),
+            pl.BlockSpec((tile, cols), lambda i: (i, 0)),
+            whole((8, width, part)),
+            pl.BlockSpec((2, width, part), lambda i: (i, 0, 0)),
+            whole((2, 8, CAP, part)),
+            whole((CAP, 128)),
+            whole((width, width)),
+        ],
+        out_specs=pl.BlockSpec((tile, cols), lambda i: (i, 0)),
+        scratch_shapes=[
+            pltpu.VMEM((2, width, cols), BF16),
+            pltpu.VMEM((6 * CAP, cols), BF16),
+            pltpu.VMEM((CAP, 1), jnp.int32),
+        ],
+        compiler_params=pltpu.CompilerParams(vmem_limit_bytes=48 * 1024 * 1024),
+        name="compact_update",
+    )(piv_col, piv_row, matrix, qc, qr, swaps, corner, coupling)
+
+
 def per_device(matrix, pivots, coupling):
     width = coupling.shape[0]
+    rows = matrix.shape[0]
     piv_col, piv_row = pivots.reshape(width, 1), pivots.reshape(1, width)
-    picked = pick(matrix, pivots)
-    qc, qr = exchange(picked, matrix, piv_col, piv_row)
-    return update(piv_col, piv_row, matrix, qc, qr, coupling)
+
+    def compact(matrix, pivots, coupling):
+        parts = compact_exchange(matrix, piv_col, piv_row)
+        return compact_update(piv_col, piv_row, matrix, *parts, coupling)
+
+    def general(matrix, pivots, coupling):
+        picked = pick(matrix, pivots)
+        qc, qr = exchange(picked, matrix, piv_col, piv_row)
+        return update(piv_col, piv_row, matrix, qc, qr, coupling)
+
+    blocks = jnp.arange(16, dtype=jnp.int32)[:, None]
+    counts = jnp.sum((piv_row // rows == blocks).astype(jnp.int32), axis=1)
+    return lax.cond(jnp.max(counts) <= CAP, compact, general, matrix, pivots, coupling)
 
 
 def solution(mesh):

time: 99.6 us -> 71.3 us (0.72)
  the two profiles are of different devices: /device:TPU:54 before, /device:TPU:1 now
where the time goes in v2:
time: 71.3 us; the launch traced here: 70.1 us
  Pallas kernels  64.7 us (91%)
  local copies, waits for them, and re-layouts  2.9 us (4%)
  other arithmetic  1.44 us (2%)
    pallas_call x1, Pallas kernels, compact_exchange(): pl.pallas_call(compact_kernel, out_shape=(panel, panel, jax.ShapeDtypeStr...  57 us
    pallas_call x1, Pallas kernels, compact_update(): pl.pallas_call(compact_update_kernel, grid=(rows // tile,), out_shape=jax...  7.75 us
    unnamed x2, local copies, waits for them, and re-layouts  2.01 us

profile of v2, /device:TPU:1, one launch (start us, length us, event | category | flops | bytes accessed | tf_op | source)
XLA Modules:
  0.0 70.1 jit_solution(255914226032644419)
XLA Ops:
  0.0 0.7 and_select_fusion
  0.7 0.1 convert_reduce_fusion
  0.8 0.6 reduce_max.9
  2.1 65.9 %conditional.1 = (f32[1024,1024]{1,0:T(8,128)S(1)}) conditional(s32[]{:T(128)} %convert_element_type.7, (s32[256]{0:T(256)}, f32[1024,1024]{1,0:T(8,128)}, s32[256,1]{0,1:T(1,128)}, s32[1,256]{1,0:T(1,128)}, f32[256,256]{1,0:T(8,128)}) %tuple.23, (f32[1024,1024]{1,0:T(8,128)}, s32[256,1]{0,1:T(1,128)}, s32[1,256]{1,0:T(1,128)}, ...), branch_computations={%region_2.3_spmd, %region_3.4_spmd} | conditional | bytes 22026360 | solution.py:1034
  2.1 0.0 copy-start.5
  2.1 0.0 copy-start.7
  2.1 0.9 %copy.9.piv_col = s32[256,1]{1,0:T(8,128)S(1)} copy(s32[256,1]{0,1:T(1,128)} %bitcast.8) | data formatting | bytes 2048 | tf_op jit(solution)/shard_map
  3.0 0.0 copy-start.2
  3.0 57.0 %compact_exchange.1 = (f32[8,256,128]{2,1,0:T(8,128)S(1)}, f32[8,256,128]{2,1,0:T(8,128)S(1)}, f32[2,8,32,128]{3,2,1,0:T(8,128)S(1)}, f32[32,128]{1,0:T(8,128)S(1)}) custom-call(f32[1024,1024]{1,0:T(8,128)} %get-tuple-element.35.matrix.m, s32[256,1]{1,0:T(8,128)S(1)} %copy.9.piv_col, s32[1,256]{1,0:T(1,128)} %get-tuple-element.34.piv_row), custom_call_target="tpu_custom_call" | custom-call | tf_op jit(solution)/shard_map/cond/branch_1_fun/compact_exchange/pallas_call | solution.py:879
  60.0 0.0 copy-done.5
  60.0 0.0 copy-done.7
  60.0 0.0 copy-done.2
  60.1 7.7 %compact_update.1 = f32[1024,1024]{1,0:T(8,128)S(1)} custom-call(s32[256,1]{1,0:T(8,128)S(1)} %copy.9.piv_col, s32[1,256]{1,0:T(1,128)S(1)} %copy-done.7, f32[1024,1024]{1,0:T(8,128)S(1)} %copy-done.2, f32[8,256,128]{2,1,0:T(8,128)S(1)} %get-tuple-element.36.qc, f32[8,256,128]{2,1,0:T(8,128)S(1)} %get-tuple-element.37.qr, ...), custom_call_target="tpu_custom_call" | custom-call | tf_op jit(solution)/shard_map/cond/branch_1_fun/compact_update/pallas_call | solution.py:993
  68.0 0.0 copy-start.3
  68.0 2.0 %copy-done.3 = f32[1024,1024]{1,0:T(8,128)} copy-done((f32[1024,1024]{1,0:T(8,128)}, f32[1024,1024]{1,0:T(8,128)S(1)}, u32[]{:S(2)}) %copy-start.3) | copy-done | bytes 4194328
Async XLA Ops:
  2.1 57.9 %copy-start.5 = (f32[256,256]{1,0:T(8,128)S(1)}, f32[256,256]{1,0:T(8,128)}, u32[]{:S(2)}) copy-start(f32[256,256]{1,0:T(8,128)} %get-tuple-element.40.coupling) | copy-start | bytes 786436 | tf_op jit(solution)/shard_map/cond
  2.1 57.9 %copy-start.7 = (s32[1,256]{1,0:T(1,128)S(1)}, s32[1,256]{1,0:T(1,128)}, u32[]{:S(2)}) copy-start(s32[1,256]{1,0:T(1,128)} %get-tuple-element.34.piv_row) | copy-start | bytes 3076 | tf_op jit(solution)/shard_map/cond
  3.0 57.0 %copy-start.2 = (f32[1024,1024]{1,0:T(8,128)S(1)}, f32[1024,1024]{1,0:T(8,128)}, u32[]{:S(2)}) copy-start(f32[1024,1024]{1,0:T(8,128)} %get-tuple-element.35.matrix.m) | copy-start | bytes 12582916 | tf_op jit(solution)/shard_map/cond
  68.0 2.0 %copy-start.3 = (f32[1024,1024]{1,0:T(8,128)}, f32[1024,1024]{1,0:T(8,128)S(1)}, u32[]{:S(2)}) copy-start(f32[1024,1024]{1,0:T(8,128)S(1)} %get-tuple-element.62) | copy-start | bytes 12582916

commit v3 on v2

--- a/solution.py
+++ b/solution.py
@@ -467,15 +467,17 @@
     return jnp.bitwise_and(block, 1) * 8 + jnp.right_shift(block, 1)
 
 
-def places(piv_col, piv_row, rows):
-    width = piv_col.shape[0]
+def column(row):
+    return jnp.broadcast_to(row, (8, row.shape[1])).T[:, :1]
+
+
+def places(piv_row, rows):
+    width = piv_row.shape[1]
     first = lax.broadcasted_iota(jnp.int32, (width, width), 0)
     second = lax.broadcasted_iota(jnp.int32, (width, width), 1)
-    block_col, block_row = blocks_of(piv_col, rows), blocks_of(piv_row, rows)
-    same = block_col == block_row
-    rank_col = jnp.sum(jnp.where(same & (second < first), 1, 0), axis=1, keepdims=True)
-    rank_row = jnp.sum(jnp.where(same & (first < second), 1, 0), axis=0, keepdims=True)
-    return block_col * CAP + rank_col, block_row * CAP + rank_row
+    block_row = blocks_of(piv_row, rows)
+    before = (column(block_row) == block_row) & (first < second)
+    return block_row * CAP + jnp.sum(jnp.where(before, 1, 0), axis=0, keepdims=True)
 
 
 def listed(place_row, piv_row, start, count):
@@ -484,18 +486,20 @@
 
 
 def compact_kernel(
-    matrix, piv_col, piv_row, qc, qr, swaps, corner,
-    block, picked, fixed, hall, abuf, lead, piece, kout, kin, w0out, w0in, lout,
-    s_a, r_a, s_sib, r_sib, s_ld, r_ld, s_k, r_k, s_w0, r_w0, s_l, r_l,
-    s_b, r_b, s_f, s_t, r_t, s_y, s_z, r_y, local,
+    matrix, piv_row, qc, qr, swaps, corner, w1,
+    block, picked, hall, abuf, lead, piece, wbuf, w0out, w0in, lout,
+    s_a, r_a, s_sib, r_sib, s_ld, r_ld, s_k, r_k, s_w0, r_w0, s_w, r_w, s_l, r_l,
+    s_b, s_x, r_b, s_f, s_t, r_t, s_z, r_z, s_y, s_r, r_y, local,
 ):
     r, c = lax.axis_index("row"), lax.axis_index("col")
     rows, cols = matrix.shape
-    width = piv_col.shape[0]
+    width = piv_row.shape[1]
     half, part = width // 2, cols // 8
     q, core = lax.div(r, 2), lax.rem(r, 2)
-    x, y, zh = lax.div(r, 4), lax.div(c, 4), lax.rem(c, 4)
+    zl = lax.rem(q, 2)
+    y, zh = lax.div(c, 4), lax.rem(c, 4)
     sib = r + 1 - 2 * core
+    pair = q + 1 - 2 * zl
     chunk = lax.div(order(c), 4)
 
     def remote(src, dst, ssem, rsem, row, col):
@@ -513,8 +517,10 @@
     def sent(copy):
         copy.wait_send()
 
-    def dot(a, b):
-        return jnp.dot(a, b, precision=HIGHEST, preferred_element_type=F32)
+    def dot(a, b, dims=((1,), (0,))):
+        return lax.dot_general(
+            a, b, (dims, ((), ())), precision=HIGHEST, preferred_element_type=F32
+        )
 
     load = pltpu.make_async_copy(matrix, block, local.at[0])
     load.start()
@@ -528,10 +534,12 @@
         signal(lax.rem(r + d, 16), c)
     for d in (1, 3):
         signal(r, lax.rem(y + d, 4) * 4 + zh)
-    for j in range(4):
-        @pl.when((r != c) | (4 * y + j != r))
-        def _():
-            signal(4 * y + j, r)
+    for d in (1, 2, 3):
+        signal(r, 4 * y + lax.rem(zh + d, 4))
+
+    @pl.when(r != c)
+    def _():
+        signal(c, r)
 
     @pl.when(c != 0)
     def _():
@@ -547,73 +555,60 @@
         for j in range(8):
             signal(2 * j + lax.rem(c, 2), r)
 
-    greeted = 15 + 2 + 4 - jnp.where(r == c, 1, 0) + jnp.where(c == 0, 15, 1)
+    greeted = 15 + 2 + 3 + jnp.where(r == c, 0, 1) + jnp.where(c == 0, 15, 1)
     greeted = greeted + lax.div(c - core + 1, 2)
 
-    place_col, place_row = places(piv_col[...], piv_row[...], rows)
+    place_row = places(piv_row[...], rows)
     spots = lax.broadcasted_iota(jnp.int32, (16 * CAP, width), 0)
     hall[...] = (spots == place_row).astype(F32)
     mine = order(r) * CAP
     have = listed(place_row, piv_row[...], mine, CAP) >= 0
+    here_piv = listed(place_row, piv_row[...], chunk * 128, 128)
     load.wait()
     for t in range(CAP):
         local_row = jnp.sum(jnp.where(place_row == mine + t, piv_row[...] - r * rows, 0))
         picked[pl.ds(t, 1)] = block[pl.ds(jnp.clip(local_row, 0, rows - 1), 1)]
     picked[...] = jnp.where(have, picked[...], 0.0)
 
+    @pl.when(c == 0)
+    def _():
+        wbuf[core, q] = picked[:, :width]
+
     pl.semaphore_wait(barrier, greeted)
 
-    def lead_copy(p):
-        return remote(
-            block.at[pl.ds(0, width), pl.ds(p * part, part)], lead, s_ld.at[p], r_ld.at[0], 2 * p, c
-        )
-
-    @pl.when(r == 0)
-    def _():
-        for p in range(1, 8):
-            lead_copy(p).start()
-
-    here_piv = listed(place_row, piv_row[...], chunk * 128, 128)
-    spread = one_hot(here_piv, c * cols, (128, cols), 1).astype(F32)
-    swapped = jnp.max(spread, axis=0, keepdims=True) > 0
+    def a_copy(d):
+        p = lax.rem(q + d, 8)
+        cut = pl.ds(pl.multiple_of(p * part, part), part)
+        return p, remote(picked.at[:, cut], abuf.at[core, q], s_a.at[d], r_a.at[q], 2 * p + core, c)
+
+    for d in range(1, 8):
+        p, copy = a_copy(d)
+
+        @pl.when((c != 0) | (p >= width // part))
+        def _():
+            copy.start()
 
     def k_copy(i, b):
-        return remote(
-            kout.at[i, lax.div(order(b), 4)], kin.at[i], s_k.at[i, b], r_k.at[i], r, b
-        )
+        src = wbuf.at[core, q] if i == 0 else corner
+        return remote(src, src, s_k.at[i, b], r_k.at[i], r, b)
 
     def k_copies(i, act):
         for b in range(1, 16):
             act(k_copy(i, b))
 
-    def k_lists(i, value):
-        compact = lax.dot_general(
-            value, hall[...], (((1,), (1,)), ((), ())),
-            precision=HIGHEST, preferred_element_type=F32,
-        )
-        for j in range(4):
-            kout[i, j] = compact[:, 128 * j : 128 * (j + 1)]
+    @pl.when(c == 0)
+    def _():
+        k_copies(0, start)
 
     def w0_copy(b):
         return remote(w0out, w0in.at[b], s_w0.at[0], r_w0.at[b], r, 0)
 
-    @pl.when(c == 0)
-    def _():
-        k_lists(0, picked[:, :width])
-        k_copies(0, start)
-        kin[0] = kout[0, 0]
-
-    w0out[...] = lax.dot_general(
-        picked[...], spread, (((1,), (1,)), ((), ())),
-        precision=HIGHEST, preferred_element_type=F32,
-    )
+    spread = one_hot(here_piv, c * cols, (128, cols), 1).astype(F32)
+    w0out[...] = dot(picked[...], spread, ((1,), (1,)))
 
     @pl.when(c != 0)
     def _():
         w0_copy(c).start()
-        arrived(kin.at[0], r_k.at[0])
-
-    fixed[...] = jnp.where(swapped, dot(kin[0], spread), picked[...])
 
     @pl.when(c == 0)
     def _():
@@ -626,30 +621,25 @@
                 w0in[b] for b in range(16) if ((b % 2) * 8 + b // 2) // 4 == j
             )
             total = total + dot(listing, hall[128 * j : 128 * (j + 1)])
-        fixed[:, :width] = total
-
-    def a_copy(d):
-        p = lax.rem(q + d, 8)
-        cut = pl.ds(pl.multiple_of(p * part, part), part)
-        return remote(fixed.at[:, cut], abuf.at[core, q], s_a.at[d], r_a.at[q], 2 * p + core, c)
-
-    for d in range(1, 8):
-        a_copy(d).start()
-    abuf[core, q] = fixed[:, pl.ds(pl.multiple_of(q * part, part), part)]
-
-    lead_sib = remote(lead, lead, s_sib.at[0], r_sib.at[0], sib, c)
+        picked[:, :width] = total
+        for d in range(1, 8):
+            p, copy = a_copy(d)
+
+            @pl.when(p < width // part)
+            def _():
+                copy.start()
+
+    abuf[core, q] = picked[:, pl.ds(pl.multiple_of(q * part, part), part)]
+
+    def lead_copy(p):
+        return remote(
+            block.at[pl.ds(0, width), pl.ds(p * part, part)], lead, s_ld.at[p], r_ld.at[0], 2 * p, c
+        )
 
     @pl.when(r == 0)
     def _():
-        lead[...] = block[:width, :part]
-
-    @pl.when((core == 0) & (r != 0))
-    def _():
-        arrived(lead, r_ld.at[0])
-
-    @pl.when(core == 0)
-    def _():
-        lead_sib.start()
+        for p in range(1, 8):
+            lead_copy(p).start()
 
     for d in range(1, 8):
         p = lax.rem(q + d, 8)
@@ -659,52 +649,157 @@
     arrived(abuf.at[1 - core], r_sib.at[1])
 
     lay = jnp.where(core == 0, hall[:, :half], hall[:, half:])
-    piece[...] = lax.dot_general(
-        lay, abuf[...].reshape(16 * CAP, part), (((0,), (0,)), ((), ())),
-        precision=HIGHEST, preferred_element_type=F32,
-    )
+    piece[...] = dot(lay, abuf[...].reshape(16 * CAP, part), ((0,), (0,)))
 
     def slot(k):
         return pl.ds(pl.multiple_of(k * half, half), half)
 
-    def t_copies(act, act_here):
-        for k in range(4):
-            here = (r == c) & (k == zh)
-
-            @pl.when(jnp.logical_not(here))
-            def _():
-                act(
-                    remote(
-                        piece, qr.at[q, slot(core)], s_t.at[k], r_t.at[lax.rem(r, 4)], c, 4 * x + k
-                    )
-                )
-
-            @pl.when(here)
-            def _():
-                act_here(pltpu.make_async_copy(piece, qr.at[q, slot(core)], local.at[1]))
+    t_copy = remote(piece, qr.at[q, slot(core)], s_t.at[0], r_t.at[0], c, r)
+    t_here = pltpu.make_async_copy(piece, qr.at[q, slot(core)], local.at[1])
+
+    @pl.when(r != c)
+    def _():
+        t_copy.start()
+
+    @pl.when(r == c)
+    def _():
+        t_here.start()
+
+    def wanted(p):
+        return 2 * p + 1 >= c
 
     def b_copies(act):
-        for d in range(1, 8):
-            p = lax.rem(q + d, 8)
-
-            @pl.when(2 * p + 1 >= c)
+        @pl.when(wanted(6 + 1 - zl))
+        def _():
+            act(
+                remote(piece, qc.at[q, slot(core)], s_b.at[0], r_b.at[core, q], 2 * pair + core, c)
+            )
+
+        for d in range(1, 4):
+            p = lax.rem(q + 2 * d, 8)
+
+            @pl.when(wanted(p))
             def _():
                 act(remote(piece, qc.at[q, slot(core)], s_b.at[d], r_b.at[core, q], 2 * p + core, c))
+
+    def x_copies(act):
+        for d in range(1, 4):
+            p = lax.rem(q + 2 * d, 8)
+            ref = qc.at[pair, slot(core)]
+
+            @pl.when(wanted(p))
+            def _():
+                act(remote(ref, ref, s_x.at[d], r_b.at[core, pair], 2 * p + core, c))
 
     def f_copy(d):
         p = lax.rem(q + d, 8)
         src = piece if d == 0 else qc.at[p, slot(core)]
         return remote(src, qc.at[p, slot(core)], s_f.at[d], r_b.at[core, p], sib, c)
 
-    t_copies(start, start)
+    b_copies(start)
 
     @pl.when(sib >= c)
     def _():
         f_copy(0).start()
 
-    b_copies(start)
     keep = pltpu.make_async_copy(piece, qc.at[q, slot(core)], local.at[2])
     keep.start()
+
+    def w_copies(act):
+        for d in range(1, 8):
+            p = lax.rem(q + d, 8)
+
+            @pl.when(wanted(p))
+            def _():
+                act(
+                    remote(
+                        wbuf.at[core, q], wbuf.at[core, q], s_w.at[d], r_w.at[q], 2 * p + core, c
+                    )
+                )
+
+    @pl.when(c != 0)
+    def _():
+        arrived(wbuf.at[core, q], r_k.at[0])
+
+    w_copies(start)
+
+    lead_sib = remote(lead, lead, s_sib.at[0], r_sib.at[0], sib, c)
+
+    @pl.when(r == 0)
+    def _():
+        lead[...] = block[:width, :part]
+
+    @pl.when((core == 0) & (r != 0))
+    def _():
+        arrived(lead, r_ld.at[0])
+
+    @pl.when(core == 0)
+    def _():
+        lead_sib.start()
+
+    def need(there):
+        return 4 * there + zh <= r
+
+    up, down, across = lax.rem(y + 1, 4), lax.rem(y + 3, 4), lax.rem(y + 2, 4)
+
+    def y_ref(owner, k):
+        j = lax.rem(zh + k, 4)
+        return qr.at[2 * owner + lax.div(j, 2), slot(lax.rem(j, 2))]
+
+    def z_copies(act):
+        for d in (1, 3, 2):
+            there = lax.rem(zh + d, 4)
+
+            @pl.when(there <= r)
+            def _():
+                act(
+                    remote(
+                        y_ref(y, 0), y_ref(y, 0), s_z.at[d], r_z.at[(4 - d) % 4], r, 4 * y + there
+                    )
+                )
+
+    def y_copies(k, act):
+        onward = need(across)
+
+        def one(way, to):
+            ref = y_ref(y, k)
+            act(remote(ref, ref, s_y.at[way, k], r_y.at[y, k], r, 4 * to + zh))
+
+        @pl.when(need(up) | onward if k % 2 == 0 else need(up))
+        def _():
+            one(0, up)
+
+        @pl.when(need(down) | onward if k % 2 == 1 else need(down))
+        def _():
+            one(1, down)
+
+    def relay(k, act):
+        owner, to = (down, up) if k % 2 == 0 else (up, down)
+        ref = y_ref(owner, k)
+
+        @pl.when(need(to))
+        def _():
+            act(remote(ref, ref, s_r.at[k], r_y.at[owner, k], r, 4 * to + zh))
+
+    def run_relay(k):
+        owner, to = (down, up) if k % 2 == 0 else (up, down)
+
+        @pl.when(need(y) | need(to))
+        def _():
+            arrived(y_ref(owner, k), r_y.at[owner, k])
+
+        relay(k, start)
+
+    @pl.when(r != c)
+    def _():
+        arrived(y_ref(y, 0), r_t.at[0])
+
+    @pl.when(r == c)
+    def _():
+        t_here.wait()
+
+    y_copies(0, start)
+    z_copies(start)
 
     @pl.when(core == 1)
     def _():
@@ -718,14 +813,12 @@
             s = 2 * j + core
             as_row = s >= c
             row, col = jnp.where(as_row, s, c), jnp.where(as_row, c, s)
-            dst = swaps.at[jnp.where(as_row, 0, 1), q]
+            kind = jnp.where(as_row, 0, 1)
             here = as_row & (s == r)
 
             @pl.when(jnp.logical_not(here))
             def _():
-                act(
-                    remote(lout.at[j], dst, s_l.at[j], r_l.at[jnp.where(as_row, 0, 1), q], row, col)
-                )
+                act(remote(lout.at[j], swaps.at[kind, q], s_l.at[j], r_l.at[kind, q], row, col))
 
             @pl.when(here)
             def _():
@@ -736,53 +829,28 @@
 
     l_copies(start, keep_lead)
 
-    def need(there):
-        return 4 * there + zh <= r
-
-    up, down, across = lax.rem(y + 1, 4), lax.rem(y + 3, 4), lax.rem(y + 2, 4)
-
-    def y_ref(owner, j):
-        return qr.at[2 * owner + j // 2, slot(j % 2)]
-
-    def y_copy(j, way):
-        col = (up if way == 0 else down) * 4 + zh
-        return remote(y_ref(y, j), y_ref(y, j), s_y.at[way, j], r_y.at[y, j], r, col)
-
-    def z_copy(j):
-        owner, to = (down, up) if j < 2 else (up, down)
-        return remote(y_ref(owner, j), y_ref(owner, j), s_z.at[j], r_y.at[owner, j], r, 4 * to + zh)
-
-    def y_copies(j, act):
-        on_up = need(up) | need(across) if j < 2 else need(up)
-        on_down = need(down) | need(across) if j >= 2 else need(down)
-
-        @pl.when(on_up)
-        def _():
-            act(y_copy(j, 0))
-
-        @pl.when(on_down)
-        def _():
-            act(y_copy(j, 1))
-
-    def z_copies(j, act):
-        @pl.when(need(up) if j < 2 else need(down))
-        def _():
-            act(z_copy(j))
-
-    for j in range(4):
-        here = (r == c) & (4 * y + j == r)
-
-        @pl.when(jnp.logical_not(here))
-        def _():
-            arrived(y_ref(y, j), r_t.at[j])
-
-        @pl.when(here)
-        def _():
-            pltpu.make_async_copy(piece, qr.at[q, slot(core)], local.at[1]).wait()
-
-        y_copies(j, start)
-
-    @pl.when((r >= c))
+    def run_y(k):
+        @pl.when(zh <= r)
+        def _():
+            arrived(y_ref(y, k), r_z.at[k])
+
+        y_copies(k, start)
+
+    run_relay(0)
+    run_y(1)
+    run_y(3)
+    run_relay(1)
+    run_relay(3)
+    run_y(2)
+
+    @pl.when(wanted(6 + zl))
+    def _():
+        arrived(qc.at[pair, slot(core)], r_b.at[core, pair])
+
+    x_copies(start)
+    run_relay(2)
+
+    @pl.when(r >= c)
     def _():
         for p in range(8):
             @pl.when(p != q)
@@ -791,38 +859,46 @@
 
     @pl.when(c == 0)
     def _():
-        k_lists(1, jnp.concatenate([swaps[0, p] for p in range(width // part)], axis=1))
+        for p in range(width // part):
+            corner[:, p * part : (p + 1) * part] = swaps[0, p]
         k_copies(1, start)
-        kin[1] = kout[1, 0]
-
-    for j in (0, 1, 2, 3):
-        owner = down if j < 2 else up
-
-        @pl.when(need(y) | (need(up) if j < 2 else need(down)))
-        def _():
-            arrived(y_ref(owner, j), r_y.at[owner, j])
-
-        z_copies(j, start)
+
+    @pl.when(wanted(q))
+    def _():
+        for d in range(1, 8):
+            p = lax.rem(q + d, 8)
+            arrived(wbuf.at[core, p], r_w.at[p])
+
+    w_sib = remote(wbuf.at[core], wbuf.at[core], s_sib.at[2], r_sib.at[2], sib, c)
+
+    @pl.when(sib >= c)
+    def _():
+        w_sib.start()
 
     for d in range(1, 8):
         p = lax.rem(q + d, 8)
 
-        @pl.when(2 * q + 1 >= c)
+        @pl.when(wanted(q) & (p != pair))
         def _():
             arrived(qc.at[p, slot(core)], r_b.at[core, p])
 
         @pl.when(sib >= c)
         def _():
             f_copy(d).start()
+
+    @pl.when(r >= c)
+    def _():
+        arrived(wbuf.at[1 - core], r_sib.at[2])
+        w1[...] = dot(hall[...], wbuf[...].reshape(16 * CAP, width), ((0,), (0,)))
 
     @pl.when(r >= c)
     def _():
         for p in range(8):
             arrived(qc.at[p, slot(1 - core)], r_b.at[1 - core, p])
-        for j in range(4):
-            owner = up if j < 2 else down
-            arrived(y_ref(owner, j), r_y.at[owner, j])
-            arrived(y_ref(across, j), r_y.at[across, j])
+        for k in range(4):
+            owner = up if k % 2 == 0 else down
+            arrived(y_ref(owner, k), r_y.at[owner, k])
+            arrived(y_ref(across, k), r_y.at[across, k])
 
     @pl.when(r > c)
     def _():
@@ -831,10 +907,9 @@
 
     @pl.when(c != 0)
     def _():
-        arrived(kin.at[1], r_k.at[1])
+        arrived(corner, r_k.at[1])
         w0_copy(c).wait_send()
 
-    corner[...] = kin[1]
     keep.wait()
 
     @pl.when(r == 0)
@@ -848,29 +923,36 @@
 
     a_sib.wait_send()
     for d in range(1, 8):
-        a_copy(d).wait_send()
+        a_copy(d)[1].wait_send()
 
     @pl.when(c == 0)
     def _():
         k_copies(0, sent)
         k_copies(1, sent)
 
-    t_copies(sent, lambda copy: None)
+    @pl.when(r != c)
+    def _():
+        t_copy.wait_send()
+
     b_copies(sent)
+    x_copies(sent)
+    w_copies(sent)
+    z_copies(sent)
     l_copies(sent, lambda j: None)
-    for j in range(4):
-        y_copies(j, sent)
-        z_copies(j, sent)
+    for k in range(4):
+        y_copies(k, sent)
+        relay(k, sent)
 
     @pl.when(sib >= c)
     def _():
+        w_sib.wait_send()
         for d in range(8):
             f_copy(d).wait_send()
 
 
-def compact_exchange(matrix, piv_col, piv_row):
+def compact_exchange(matrix, piv_row):
     rows, cols = matrix.shape
-    width = piv_col.shape[0]
+    width = piv_row.shape[1]
     half, part = width // 2, cols // 8
     dma = pltpu.SemaphoreType.DMA
     any_spec = pl.BlockSpec(memory_space=pl.ANY)
@@ -882,40 +964,41 @@
             panel,
             panel,
             jax.ShapeDtypeStruct((2, 8, CAP, part), F32),
-            jax.ShapeDtypeStruct((CAP, 128), F32),
+            jax.ShapeDtypeStruct((CAP, width), F32),
+            jax.ShapeDtypeStruct((width, width), F32),
         ),
-        in_specs=[any_spec, vmem, vmem],
-        out_specs=(any_spec, any_spec, vmem, vmem),
+        in_specs=[any_spec, vmem],
+        out_specs=(any_spec, any_spec, vmem, vmem, vmem),
         scratch_shapes=[
             pltpu.VMEM((rows, cols), F32),
-            pltpu.VMEM((CAP, cols), F32),
             pltpu.VMEM((CAP, cols), F32),
             pltpu.VMEM((16 * CAP, width), F32),
             pltpu.VMEM((2, 8, CAP, part), F32),
             pltpu.VMEM((width, part), F32),
             pltpu.VMEM((half, part), F32),
-            pltpu.VMEM((2, 4, CAP, 128), F32),
-            pltpu.VMEM((2, CAP, 128), F32),
+            pltpu.VMEM((2, 8, CAP, width), F32),
             pltpu.VMEM((CAP, 128), F32),
             pltpu.VMEM((16, CAP, 128), F32),
             pltpu.VMEM((8, CAP, part), F32),
-            dma((8,)), dma((8,)), dma((2,)), dma((2,)), dma((8,)), dma((1,)),
-            dma((2, 16)), dma((2,)), dma((1,)), dma((16,)), dma((8,)), dma((2, 8)),
-            dma((8,)), dma((2, 8)), dma((8,)), dma((4,)), dma((4,)), dma((2, 4)), dma((4,)), dma((4, 4)),
+            dma((8,)), dma((8,)), dma((3,)), dma((3,)), dma((8,)), dma((1,)),
+            dma((2, 16)), dma((2,)), dma((1,)), dma((16,)), dma((8,)), dma((8,)), dma((8,)), dma((2, 8)),
+            dma((4,)), dma((4,)), dma((2, 8)), dma((8,)), dma((1,)), dma((1,)), dma((4,)), dma((4,)),
+            dma((2, 4)), dma((4,)), dma((4, 4)),
             dma((3,)),
         ],
         compiler_params=pltpu.CompilerParams(
             collective_id=1, has_side_effects=True, vmem_limit_bytes=32 * 1024 * 1024
         ),
         name="compact_exchange",
-    )(matrix, piv_col, piv_row)
+    )(matrix, piv_row)
 
 
 def compact_update_kernel(
-    piv_col, piv_row, m, qc, qr, swaps, corner, coupling, out, panel, right, left
+    piv_row, m, qc, qr, swaps, corner, w1, coupling, result, panel, right, left, piv_col, w1s,
+    outs, sems,
 ):
     r, c = lax.axis_index("row"), lax.axis_index("col")
-    tile, cols = out.shape
+    tile, cols = m.shape
     rows = tile * pl.num_programs(0)
     width = coupling.shape[0]
     part = qc.shape[2]
@@ -923,8 +1006,20 @@
     row_start = r * rows + step * tile
     col_start = c * cols
 
-    def dot(a, b):
-        return lax.dot_general(a, b, (((0,), (0,)), ((), ())), preferred_element_type=F32)
+    def dot(a, b, dims=((0,), (0,))):
+        return lax.dot_general(a, b, (dims, ((), ())), preferred_element_type=F32)
+
+    across = ((1,), (0,))
+    slot = lax.rem(step, 2)
+    out = outs.at[slot]
+
+    def put(i):
+        at = pl.ds(pl.multiple_of(i * tile, tile), tile)
+        return pltpu.make_async_copy(outs.at[lax.rem(i, 2)], result.at[at], sems.at[lax.rem(i, 2)])
+
+    @pl.when(step >= 2)
+    def _():
+        put(step - 2).wait()
 
     @pl.when(r < c)
     def _():
@@ -932,16 +1027,22 @@
 
     @pl.when((r >= c) & (step == 0))
     def _():
-        _, place_row = places(piv_col[...], piv_row[...], rows)
+        place_row = places(piv_row[...], rows)
+        piv_col[...] = column(piv_row[...])
+        spread = one_hot(piv_col[...], col_start, (width, cols), 1).astype(F32)
+        hit = jnp.max(spread, axis=0, keepdims=True) > 0
+        spread = spread.astype(BF16)
+        for i, term in enumerate(split(w1[...], 3)):
+            w1s[i] = term
+        placed = [dot(w1s[i], spread, across) for i in range(2)]
         for i in range(8):
+            cut = slice(i * part, (i + 1) * part)
             for j, term in enumerate(split(qc[i], 2)):
-                panel[j, :, i * part : (i + 1) * part] = term
-        here_piv = listed(place_row, piv_row[...], lax.div(order(c), 4) * 128, 128)
-        spread = one_hot(here_piv, col_start, (128, cols), 1).astype(F32)
-        swapped = jnp.max(spread, axis=0, keepdims=True) > 0
+                term = jnp.where(hit[:, cut], placed[j][:, cut], term.astype(F32))
+                panel[j, :, cut] = term.astype(BF16)
         lead = jnp.concatenate([swaps[0, i] for i in range(8)], axis=1)
-        placed = jnp.dot(corner[...], spread, precision=HIGHEST, preferred_element_type=F32)
-        lead = jnp.where(swapped, placed, lead)
+        placed = sum(dot(term, spread, across) for term in split(corner[...], 3))
+        lead = jnp.where(hit, placed, lead)
         for j, term in enumerate(split(lead, 3)):
             right[j * CAP : (j + 1) * CAP] = term
         col_piv = listed(place_row, piv_row[...], order(c) * CAP, CAP)
@@ -952,22 +1053,25 @@
 
     @pl.when(r >= c)
     def _():
+        hot = one_hot(left[...], row_start, (CAP, tile), 1).astype(F32)
+        hit = jnp.max(hot, axis=0, keepdims=True)
         rows_t = jnp.concatenate([qr[0], qr[1]], axis=1)
+        spread = one_hot(piv_col[...], row_start, (width, tile), 1).astype(F32).astype(BF16)
+        placed = sum(dot(w1s[i], spread, across) for i in range(3))
+        rows_t = jnp.where(hit > 0, placed, rows_t)
         scaled = lax.dot_general(
             coupling[...], rows_t, (((0,), (0,)), ((), ())),
             precision=HIGHEST, preferred_element_type=F32,
         )
         s_hi, s_lo = split(scaled, 2)
         change = dot(s_hi, panel[0]) + dot(s_hi, panel[1]) + dot(s_lo, panel[0])
-        hot = one_hot(left[...], row_start, (CAP, tile), 1).astype(F32)
-        hit = jnp.max(hot, axis=0, keepdims=True)
         which = jnp.where(r == c, 0, 1)
         lead = jnp.concatenate([swaps[which, 2 * step + i] for i in range(2)], axis=1)
         lead = jnp.where(hit > 0, 0.0, lead)
         hot = hot.astype(BF16)
         lhs = jnp.concatenate([hot, hot, hot] + split(lead, 3), axis=0)
         moved = dot(lhs, right[...])
-        hit_row = jnp.broadcast_to(hit, (8, tile)).T[:, :1] > 0
+        hit_row = column(hit) > 0
         hit_col = jnp.max(right[3 * CAP : 4 * CAP].astype(F32), axis=0, keepdims=True) > 0
         value = jnp.where(hit_row | hit_col, 0.0, m[...]) + moved
         places_col = lax.broadcasted_iota(jnp.int32, (tile, cols), 1) + col_start
@@ -980,8 +1084,15 @@
                 below[:, :width], rows_t.T - change[:, :width], 0.0
             )
 
-
-def compact_update(piv_col, piv_row, matrix, qc, qr, swaps, corner, coupling):
+    put(step).start()
+
+    @pl.when(step == pl.num_programs(0) - 1)
+    def _():
+        put(step - 1).wait()
+        put(step).wait()
+
+
+def compact_update(piv_row, matrix, qc, qr, swaps, corner, w1, coupling):
     rows, cols = matrix.shape
     width = coupling.shape[0]
     part = cols // 8
@@ -995,36 +1106,41 @@
         grid=(rows // tile,),
         out_shape=jax.ShapeDtypeStruct((rows, cols), F32),
         in_specs=[
-            whole((width, 1)),
             whole((1, width)),
             pl.BlockSpec((tile, cols), lambda i: (i, 0)),
             whole((8, width, part)),
             pl.BlockSpec((2, width, part), lambda i: (i, 0, 0)),
             whole((2, 8, CAP, part)),
-            whole((CAP, 128)),
+            whole((CAP, width)),
+            whole((width, width)),
             whole((width, width)),
         ],
-        out_specs=pl.BlockSpec((tile, cols), lambda i: (i, 0)),
+        out_specs=pl.BlockSpec(memory_space=pltpu.HBM),
         scratch_shapes=[
             pltpu.VMEM((2, width, cols), BF16),
             pltpu.VMEM((6 * CAP, cols), BF16),
             pltpu.VMEM((CAP, 1), jnp.int32),
+            pltpu.VMEM((width, 1), jnp.int32),
+            pltpu.VMEM((3, width, width), BF16),
+            pltpu.VMEM((2, tile, cols), F32),
+            pltpu.SemaphoreType.DMA((2,)),
         ],
-        compiler_params=pltpu.CompilerParams(vmem_limit_bytes=48 * 1024 * 1024),
+        compiler_params=pltpu.CompilerParams(vmem_limit_bytes=32 * 1024 * 1024),
         name="compact_update",
-    )(piv_col, piv_row, matrix, qc, qr, swaps, corner, coupling)
+    )(piv_row, matrix, qc, qr, swaps, corner, w1, coupling)
 
 
 def per_device(matrix, pivots, coupling):
     width = coupling.shape[0]
     rows = matrix.shape[0]
-    piv_col, piv_row = pivots.reshape(width, 1), pivots.reshape(1, width)
+    piv_row = pivots.reshape(1, width)
 
     def compact(matrix, pivots, coupling):
-        parts = compact_exchange(matrix, piv_col, piv_row)
-        return compact_update(piv_col, piv_row, matrix, *parts, coupling)
+        parts = compact_exchange(matrix, piv_row)
+        return compact_update(piv_row, matrix, *parts, coupling)
 
     def general(matrix, pivots, coupling):
+        piv_col = pivots.reshape(width, 1)
         picked = pick(matrix, pivots)
         qc, qr = exchange(picked, matrix, piv_col, piv_row)
         return update(piv_col, piv_row, matrix, qc, qr, coupling)

time: 71.3 us -> 63.3 us (0.89); the launches traced: 70.1 us -> 63 us
  Pallas kernels: 64.7 us -> 58.6 us
  local copies, waits for them, and re-layouts: 2.9 us -> 2.02 us
    pallas_call x1, Pallas kernels: 57 us -> 47.8 us  [compact_exchange(): pl.pallas_call(compact_kernel, out_shape=(panel, panel, jax.ShapeDtypeStr...]
    pallas_call x1, Pallas kernels: 7.75 us -> 10.8 us  [compact_update(): pl.pallas_call(compact_update_kernel, grid=(rows // tile,), out_shape=jax...]
    another operation x1 -> x0, local copies, waits for them, and re-layouts: 0.87 us -> none
where the time goes in v3:
time: 63.3 us; the launch traced here: 63 us
  Pallas kernels  58.6 us (93%)
  local copies, waits for them, and re-layouts  2.02 us (3%)
  other arithmetic  1.44 us (2%)
  between operations  0.67 us (1%)
    pallas_call x1, Pallas kernels, compact_exchange(): pl.pallas_call(compact_kernel, out_shape=(panel, panel, jax.ShapeDtypeStr...  47.8 us
    pallas_call x1, Pallas kernels, compact_update(): pl.pallas_call(compact_update_kernel, grid=(rows // tile,), out_shape=jax...  10.8 us
    unnamed x2, local copies, waits for them, and re-layouts  2.01 us

profile of v3, /device:TPU:1, one launch (start us, length us, event | category | flops | bytes accessed | tf_op | source)
XLA Modules:
  0.0 63.0 jit_solution(2407588325476140139)
XLA Ops:
  0.0 0.7 %and_select_fusion = s32[256]{0:T(256)S(1)} fusion(s32[256]{0:T(256)} %param.6), kind=kLoop, calls=%fused_computation.2 | loop fusion | flops 3840 | bytes 2048 | tf_op jit(solution)/shard_map/jit(floor_divide)/jit(_where)/select_n | solution.py:1149
  0.7 0.1 convert_reduce_fusion
  0.8 0.6 %reduce_max.9 = s32[]{:T(128)} reduce(s32[16]{0:T(128)S(1)} %convert_reduce_fusion, s32[]{:T(128)} %constant.19.clone.1), dimensions={0}, to_apply=%region_1.2 | reduce | flops 15 | bytes 72 | tf_op jit(solution)/shard_map/reduce_max | solution.py:1150
  2.1 58.9 %conditional.1 = (f32[1024,1024]{1,0:T(8,128)S(1)}) conditional(s32[]{:T(128)} %convert_element_type.7, (s32[256]{0:T(256)}, f32[1024,1024]{1,0:T(8,128)}, s32[1,256]{1,0:T(1,128)}, f32[256,256]{1,0:T(8,128)}) %tuple.18, (f32[1024,1024]{1,0:T(8,128)}, s32[1,256]{1,0:T(1,128)}, f32[256,256]{1,0:T(8,128)}) %tuple.19), branch_computations={%region_2.3_spmd, %region_3.4_spmd} | conditional | bytes 22026360 | solution.py:1150
  2.1 0.0 copy-start.2
  2.1 0.0 copy-start.6
  2.1 47.8 %compact_exchange.1 = (f32[8,256,128]{2,1,0:T(8,128)S(1)}, f32[8,256,128]{2,1,0:T(8,128)S(1)}, f32[2,8,32,128]{3,2,1,0:T(8,128)S(1)}, f32[32,256]{1,0:T(8,128)S(1)}, f32[256,256]{1,0:T(8,128)S(1)}) custom-call(f32[1024,1024]{1,0:T(8,128)} %get-tuple-element.29.matrix.m, s32[1,256]{1,0:T(1,128)} %get-tuple-element.28.piv_row), custom_call_target="tpu_custom_call" | custom-call | tf_op jit(solution)/shard_map/cond/branch_1_fun/compact_exchange/pallas_call | solution.py:961
  50.0 0.0 copy-done.2
  50.0 0.0 copy-done.6
  50.0 10.8 %compact_update.1 = f32[1024,1024]{1,0:T(8,128)S(1)} custom-call(s32[1,256]{1,0:T(1,128)S(1)} %copy-done.6, f32[1024,1024]{1,0:T(8,128)S(1)} %copy-done.2, f32[8,256,128]{2,1,0:T(8,128)S(1)} %get-tuple-element.30.qc, f32[8,256,128]{2,1,0:T(8,128)S(1)} %get-tuple-element.31.qr, f32[2,8,32,128]{3,2,1,0:T(8,128)S(1)} %get-tuple-element.32.swaps, ...), custom_call_target="tpu_custom_call" | custom-call | tf_op jit(solution)/shard_map/cond/branch_1_fun/compact_update/pallas_call | solution.py:1104
  61.0 0.0 copy-start.3
  61.0 2.0 %copy-done.3 = f32[1024,1024]{1,0:T(8,128)} copy-done((f32[1024,1024]{1,0:T(8,128)}, f32[1024,1024]{1,0:T(8,128)S(1)}, u32[]{:S(2)}) %copy-start.3) | copy-done | bytes 4194328
Async XLA Ops:
  2.1 47.9 %copy-start.2 = (f32[1024,1024]{1,0:T(8,128)S(1)}, f32[1024,1024]{1,0:T(8,128)}, u32[]{:S(2)}) copy-start(f32[1024,1024]{1,0:T(8,128)} %get-tuple-element.29.matrix.m) | copy-start | bytes 12582916 | tf_op jit(solution)/shard_map/cond
  2.1 47.9 %copy-start.6 = (s32[1,256]{1,0:T(1,128)S(1)}, s32[1,256]{1,0:T(1,128)}, u32[]{:S(2)}) copy-start(s32[1,256]{1,0:T(1,128)} %get-tuple-element.28.piv_row) | copy-start | bytes 3076 | tf_op jit(solution)/shard_map/cond
  61.0 2.0 %copy-start.3 = (f32[1024,1024]{1,0:T(8,128)}, f32[1024,1024]{1,0:T(8,128)S(1)}, u32[]{:S(2)}) copy-start(f32[1024,1024]{1,0:T(8,128)S(1)} %get-tuple-element.39) | copy-start | bytes 12582916

commit v4 on v3

--- a/solution.py
+++ b/solution.py
@@ -485,22 +485,38 @@
     return jnp.sum(jnp.where(spot == place_row, piv_row + 1, 0), axis=1, keepdims=True) - 1
 
 
+def hot16(mask):
+    return mask.astype(F32).astype(BF16)
+
+
+def dot16(a, b, dims=((1,), (0,))):
+    return lax.dot_general(a, b, (dims, ((), ())), preferred_element_type=F32)
+
+
+def choose(hot, value):
+    return sum(dot16(hot, term) for term in split(value, 3))
+
+
 def compact_kernel(
-    matrix, piv_row, qc, qr, swaps, corner, w1,
-    block, picked, hall, abuf, lead, piece, wbuf, w0out, w0in, lout,
-    s_a, r_a, s_sib, r_sib, s_ld, r_ld, s_k, r_k, s_w0, r_w0, s_w, r_w, s_l, r_l,
-    s_b, s_x, r_b, s_f, s_t, r_t, s_z, r_z, s_y, s_r, r_y, local,
+    matrix, piv_row, coupling, out,
+    block, picked, hall, hall_t, piv_col, spread, hit_col,
+    abuf, lead, piece, wbuf, vbuf, w0out, w0in, w2out, corner, lout, swaps, qc, qr,
+    w1s, w0, panel, right, left,
+    s_a, r_a, s_sib, r_sib, s_ld, r_ld, s_k, r_k, s_w0, r_w0, s_w2, r_w2, s_w, r_w, s_v, r_v,
+    s_l, r_l, s_b, s_x, r_b, s_f, s_t, r_t, s_z, r_z, s_y, s_r, r_y, local,
 ):
     r, c = lax.axis_index("row"), lax.axis_index("col")
     rows, cols = matrix.shape
     width = piv_row.shape[1]
     half, part = width // 2, cols // 8
+    tile = 2 * part
     q, core = lax.div(r, 2), lax.rem(r, 2)
     zl = lax.rem(q, 2)
     y, zh = lax.div(c, 4), lax.rem(c, 4)
     sib = r + 1 - 2 * core
     pair = q + 1 - 2 * zl
     chunk = lax.div(order(c), 4)
+    col_start = c * cols
 
     def remote(src, dst, ssem, rsem, row, col):
         return pltpu.make_async_remote_copy(
@@ -517,11 +533,6 @@
     def sent(copy):
         copy.wait_send()
 
-    def dot(a, b, dims=((1,), (0,))):
-        return lax.dot_general(
-            a, b, (dims, ((), ())), precision=HIGHEST, preferred_element_type=F32
-        )
-
     load = pltpu.make_async_copy(matrix, block, local.at[0])
     load.start()
 
@@ -530,8 +541,6 @@
     def signal(row, col):
         pl.semaphore_signal(barrier, inc=1, device_id=(row, col), device_id_type=MESH)
 
-    for d in range(1, 16):
-        signal(lax.rem(r + d, 16), c)
     for d in (1, 3):
         signal(r, lax.rem(y + d, 4) * 4 + zh)
     for d in (1, 2, 3):
@@ -555,20 +564,25 @@
         for j in range(8):
             signal(2 * j + lax.rem(c, 2), r)
 
+    for d in range(1, 16):
+        signal(lax.rem(r + d, 16), c)
+
     greeted = 15 + 2 + 3 + jnp.where(r == c, 0, 1) + jnp.where(c == 0, 15, 1)
     greeted = greeted + lax.div(c - core + 1, 2)
 
     place_row = places(piv_row[...], rows)
+    piv_col[...] = column(piv_row[...])
     spots = lax.broadcasted_iota(jnp.int32, (16 * CAP, width), 0)
-    hall[...] = (spots == place_row).astype(F32)
+    hall[...] = hot16(spots == place_row)
+    spots = lax.broadcasted_iota(jnp.int32, (width, 16 * CAP), 1)
+    hall_t[...] = hot16(spots == column(place_row))
     mine = order(r) * CAP
-    have = listed(place_row, piv_row[...], mine, CAP) >= 0
-    here_piv = listed(place_row, piv_row[...], chunk * 128, 128)
+    left[...] = listed(place_row, piv_row[...], mine, CAP)
     load.wait()
     for t in range(CAP):
         local_row = jnp.sum(jnp.where(place_row == mine + t, piv_row[...] - r * rows, 0))
         picked[pl.ds(t, 1)] = block[pl.ds(jnp.clip(local_row, 0, rows - 1), 1)]
-    picked[...] = jnp.where(have, picked[...], 0.0)
+    picked[...] = jnp.where(left[...] >= 0, picked[...], 0.0)
 
     @pl.when(c == 0)
     def _():
@@ -579,14 +593,10 @@
     def a_copy(d):
         p = lax.rem(q + d, 8)
         cut = pl.ds(pl.multiple_of(p * part, part), part)
-        return p, remote(picked.at[:, cut], abuf.at[core, q], s_a.at[d], r_a.at[q], 2 * p + core, c)
+        return remote(picked.at[:, cut], abuf.at[core, q], s_a.at[d], r_a.at[q], 2 * p + core, c)
 
     for d in range(1, 8):
-        p, copy = a_copy(d)
-
-        @pl.when((c != 0) | (p >= width // part))
-        def _():
-            copy.start()
+        a_copy(d).start()
 
     def k_copy(i, b):
         src = wbuf.at[core, q] if i == 0 else corner
@@ -600,15 +610,265 @@
     def _():
         k_copies(0, start)
 
+    def lead_copy(p):
+        return remote(
+            block.at[pl.ds(0, width), pl.ds(p * part, part)], lead, s_ld.at[p], r_ld.at[0], 2 * p, c
+        )
+
+    @pl.when(r == 0)
+    def _():
+        for p in range(1, 8):
+            lead_copy(p).start()
+
+    abuf[core, q] = picked[:, pl.ds(pl.multiple_of(q * part, part), part)]
+
+    def w2_copies(act):
+        for s in range(1, 16):
+            src = w2out.at[(s % 2) * 8 + s // 2]
+            act(remote(src, corner, s_w2.at[s], r_w2.at[0], s, 0))
+
+    @pl.when((r == 0) & (c == 0))
+    def _():
+        w2out[...] = choose(hall[...], block[:width, :width]).reshape(16, CAP, width)
+        w2_copies(start)
+        corner[...] = w2out[0]
+
     def w0_copy(b):
         return remote(w0out, w0in.at[b], s_w0.at[0], r_w0.at[b], r, 0)
 
-    spread = one_hot(here_piv, c * cols, (128, cols), 1).astype(F32)
-    w0out[...] = dot(picked[...], spread, ((1,), (1,)))
+    here_piv = listed(place_row, piv_row[...], chunk * 128, 128)
+    near = hot16(one_hot(here_piv, col_start, (128, cols), 1))
+    w0out[...] = sum(dot16(term, near, ((1,), (1,))) for term in split(picked[...], 3))
 
     @pl.when(c != 0)
     def _():
         w0_copy(c).start()
+
+    for d in range(1, 8):
+        p = lax.rem(q + d, 8)
+        arrived(abuf.at[core, p], r_a.at[p])
+    a_sib = remote(abuf.at[core], abuf.at[core], s_sib.at[1], r_sib.at[1], sib, c)
+    a_sib.start()
+    arrived(abuf.at[1 - core], r_sib.at[1])
+
+    def slot(k):
+        return pl.ds(pl.multiple_of(k * half, half), half)
+
+    piece[...] = choose(hall_t[slot(core)], abuf[...].reshape(16 * CAP, part))
+
+    t_copy = remote(piece, qr.at[q, slot(core)], s_t.at[0], r_t.at[0], c, r)
+
+    @pl.when(r != c)
+    def _():
+        t_copy.start()
+
+    @pl.when(r == c)
+    def _():
+        qr[q, slot(core)] = piece[...]
+
+    def wanted(p):
+        return 2 * p + 1 >= c
+
+    def b_copies(act):
+        @pl.when(wanted(6 + 1 - zl))
+        def _():
+            act(
+                remote(piece, qc.at[q, slot(core)], s_b.at[0], r_b.at[core, q], 2 * pair + core, c)
+            )
+
+        for d in range(1, 4):
+            p = lax.rem(q + 2 * d, 8)
+
+            @pl.when(wanted(p))
+            def _():
+                act(remote(piece, qc.at[q, slot(core)], s_b.at[d], r_b.at[core, q], 2 * p + core, c))
+
+    def x_copies(act):
+        for d in range(1, 4):
+            p = lax.rem(q + 2 * d, 8)
+            ref = qc.at[pair, slot(core)]
+
+            @pl.when(wanted(p))
+            def _():
+                act(remote(ref, ref, s_x.at[d], r_b.at[core, pair], 2 * p + core, c))
+
+    def f_copy(p):
+        ref = qc.at[p, slot(core)]
+        return remote(ref, ref, s_f.at[p], r_b.at[core, p], sib, c)
+
+    def forward(p):
+        @pl.when(sib >= c)
+        def _():
+            f_copy(p).start()
+
+    b_copies(start)
+    qc[q, slot(core)] = piece[...]
+    forward(q)
+
+    def w_copies(act, buf, ssem, rsem):
+        for d in range(1, 8):
+            p = lax.rem(q + d, 8)
+
+            @pl.when(wanted(p))
+            def _():
+                act(
+                    remote(buf.at[core, q], buf.at[core, q], ssem.at[d], rsem.at[q], 2 * p + core, c)
+                )
+
+    @pl.when(c != 0)
+    def _():
+        arrived(wbuf.at[core, q], r_k.at[0])
+
+    w_copies(start, wbuf, s_w, r_w)
+
+    lead_sib = remote(lead, lead, s_sib.at[0], r_sib.at[0], sib, c)
+
+    @pl.when(r == 0)
+    def _():
+        lead[...] = block[:width, :part]
+
+    @pl.when((core == 0) & (r != 0))
+    def _():
+        arrived(lead, r_ld.at[0])
+
+    @pl.when(core == 0)
+    def _():
+        lead_sib.start()
+
+    @pl.when(core == 1)
+    def _():
+        arrived(lead, r_sib.at[0])
+
+    lists = hall[pl.ds(pl.multiple_of(core * 8 * CAP, 8 * CAP), 8 * CAP)]
+    lout[...] = choose(lists, lead[...]).reshape(8, CAP, part)
+
+    def l_copies(act, act_here):
+        for j in range(8):
+            s = 2 * j + core
+            as_row = s >= c
+            row, col = jnp.where(as_row, s, c), jnp.where(as_row, c, s)
+            kind = jnp.where(as_row, 0, 1)
+            here = as_row & (s == r)
+
+            @pl.when(jnp.logical_not(here))
+            def _():
+                act(remote(lout.at[j], swaps.at[kind, q], s_l.at[j], r_l.at[kind, q], row, col))
+
+            @pl.when(here)
+            def _():
+                act_here(j)
+
+    def keep_lead(j):
+        swaps[0, q] = lout[j]
+
+    l_copies(start, keep_lead)
+
+    @pl.when(c == 0)
+    def _():
+        @pl.when(r != 0)
+        def _():
+            arrived(corner, r_w2.at[0])
+
+        k_copies(1, start)
+
+    hot = one_hot(piv_col[...], col_start, (width, cols), 1).astype(F32)
+    hit_col[...] = jnp.max(hot, axis=0, keepdims=True)
+    spread[...] = hot.astype(BF16)
+
+    def need(there):
+        return 4 * there + zh <= r
+
+    up, down, across = lax.rem(y + 1, 4), lax.rem(y + 3, 4), lax.rem(y + 2, 4)
+
+    def y_ref(owner, k):
+        j = lax.rem(zh + k, 4)
+        return qr.at[2 * owner + lax.div(j, 2), slot(lax.rem(j, 2))]
+
+    def z_copies(act):
+        for d in (1, 3, 2):
+            there = lax.rem(zh + d, 4)
+
+            @pl.when(there <= r)
+            def _():
+                act(
+                    remote(
+                        y_ref(y, 0), y_ref(y, 0), s_z.at[d], r_z.at[(4 - d) % 4], r, 4 * y + there
+                    )
+                )
+
+    def y_copies(k, act):
+        onward = need(across)
+
+        def one(way, to):
+            ref = y_ref(y, k)
+            act(remote(ref, ref, s_y.at[way, k], r_y.at[y, k], r, 4 * to + zh))
+
+        @pl.when(need(up) | onward if k % 2 == 0 else need(up))
+        def _():
+            one(0, up)
+
+        @pl.when(need(down) | onward if k % 2 == 1 else need(down))
+        def _():
+            one(1, down)
+
+    def relay(k, act):
+        owner, to = (down, up) if k % 2 == 0 else (up, down)
+        ref = y_ref(owner, k)
+
+        @pl.when(need(to))
+        def _():
+            act(remote(ref, ref, s_r.at[k], r_y.at[owner, k], r, 4 * to + zh))
+
+    def run_relay(k):
+        owner, to = (down, up) if k % 2 == 0 else (up, down)
+
+        @pl.when(need(y) | need(to))
+        def _():
+            arrived(y_ref(owner, k), r_y.at[owner, k])
+
+        relay(k, start)
+
+    def run_y(k):
+        @pl.when(zh <= r)
+        def _():
+            arrived(y_ref(y, k), r_z.at[k])
+
+        y_copies(k, start)
+
+    @pl.when(r != c)
+    def _():
+        arrived(y_ref(y, 0), r_t.at[0])
+
+    y_copies(0, start)
+    z_copies(start)
+
+    @pl.when(wanted(6 + zl))
+    def _():
+        arrived(qc.at[pair, slot(core)], r_b.at[core, pair])
+
+    x_copies(start)
+    forward(pair)
+    for d in range(1, 4):
+        p = lax.rem(q + 2 * d, 8)
+
+        @pl.when(wanted(q))
+        def _():
+            arrived(qc.at[p, slot(core)], r_b.at[core, p])
+
+        forward(p)
+
+    @pl.when(wanted(q))
+    def _():
+        for d in range(1, 8):
+            p = lax.rem(q + d, 8)
+            arrived(wbuf.at[core, p], r_w.at[p])
+
+    w_sib = remote(wbuf.at[core], wbuf.at[core], s_sib.at[2], r_sib.at[2], sib, c)
+    v_sib = remote(vbuf.at[core], vbuf.at[core], s_sib.at[3], r_sib.at[3], sib, c)
+
+    @pl.when(sib >= c)
+    def _():
+        w_sib.start()
 
     @pl.when(c == 0)
     def _():
@@ -620,297 +880,139 @@
             listing = sum(
                 w0in[b] for b in range(16) if ((b % 2) * 8 + b // 2) // 4 == j
             )
-            total = total + dot(listing, hall[128 * j : 128 * (j + 1)])
-        picked[:, :width] = total
-        for d in range(1, 8):
-            p, copy = a_copy(d)
-
-            @pl.when(p < width // part)
-            def _():
-                copy.start()
-
-    abuf[core, q] = picked[:, pl.ds(pl.multiple_of(q * part, part), part)]
-
-    def lead_copy(p):
-        return remote(
-            block.at[pl.ds(0, width), pl.ds(p * part, part)], lead, s_ld.at[p], r_ld.at[0], 2 * p, c
-        )
-
-    @pl.when(r == 0)
-    def _():
-        for p in range(1, 8):
-            lead_copy(p).start()
-
-    for d in range(1, 8):
-        p = lax.rem(q + d, 8)
-        arrived(abuf.at[core, p], r_a.at[p])
-    a_sib = remote(abuf.at[core], abuf.at[core], s_sib.at[1], r_sib.at[1], sib, c)
-    a_sib.start()
-    arrived(abuf.at[1 - core], r_sib.at[1])
-
-    lay = jnp.where(core == 0, hall[:, :half], hall[:, half:])
-    piece[...] = dot(lay, abuf[...].reshape(16 * CAP, part), ((0,), (0,)))
-
-    def slot(k):
-        return pl.ds(pl.multiple_of(k * half, half), half)
-
-    t_copy = remote(piece, qr.at[q, slot(core)], s_t.at[0], r_t.at[0], c, r)
-    t_here = pltpu.make_async_copy(piece, qr.at[q, slot(core)], local.at[1])
-
-    @pl.when(r != c)
-    def _():
-        t_copy.start()
-
-    @pl.when(r == c)
-    def _():
-        t_here.start()
-
-    def wanted(p):
-        return 2 * p + 1 >= c
-
-    def b_copies(act):
-        @pl.when(wanted(6 + 1 - zl))
-        def _():
-            act(
-                remote(piece, qc.at[q, slot(core)], s_b.at[0], r_b.at[core, q], 2 * pair + core, c)
-            )
-
-        for d in range(1, 4):
-            p = lax.rem(q + 2 * d, 8)
-
-            @pl.when(wanted(p))
-            def _():
-                act(remote(piece, qc.at[q, slot(core)], s_b.at[d], r_b.at[core, q], 2 * p + core, c))
-
-    def x_copies(act):
-        for d in range(1, 4):
-            p = lax.rem(q + 2 * d, 8)
-            ref = qc.at[pair, slot(core)]
-
-            @pl.when(wanted(p))
-            def _():
-                act(remote(ref, ref, s_x.at[d], r_b.at[core, pair], 2 * p + core, c))
-
-    def f_copy(d):
-        p = lax.rem(q + d, 8)
-        src = piece if d == 0 else qc.at[p, slot(core)]
-        return remote(src, qc.at[p, slot(core)], s_f.at[d], r_b.at[core, p], sib, c)
-
-    b_copies(start)
-
-    @pl.when(sib >= c)
-    def _():
-        f_copy(0).start()
-
-    keep = pltpu.make_async_copy(piece, qc.at[q, slot(core)], local.at[2])
-    keep.start()
-
-    def w_copies(act):
-        for d in range(1, 8):
-            p = lax.rem(q + d, 8)
-
-            @pl.when(wanted(p))
-            def _():
-                act(
-                    remote(
-                        wbuf.at[core, q], wbuf.at[core, q], s_w.at[d], r_w.at[q], 2 * p + core, c
-                    )
-                )
-
-    @pl.when(c != 0)
-    def _():
-        arrived(wbuf.at[core, q], r_k.at[0])
-
-    w_copies(start)
-
-    lead_sib = remote(lead, lead, s_sib.at[0], r_sib.at[0], sib, c)
-
-    @pl.when(r == 0)
-    def _():
-        lead[...] = block[:width, :part]
-
-    @pl.when((core == 0) & (r != 0))
-    def _():
-        arrived(lead, r_ld.at[0])
-
-    @pl.when(core == 0)
-    def _():
-        lead_sib.start()
-
-    def need(there):
-        return 4 * there + zh <= r
-
-    up, down, across = lax.rem(y + 1, 4), lax.rem(y + 3, 4), lax.rem(y + 2, 4)
-
-    def y_ref(owner, k):
-        j = lax.rem(zh + k, 4)
-        return qr.at[2 * owner + lax.div(j, 2), slot(lax.rem(j, 2))]
-
-    def z_copies(act):
-        for d in (1, 3, 2):
-            there = lax.rem(zh + d, 4)
-
-            @pl.when(there <= r)
-            def _():
-                act(
-                    remote(
-                        y_ref(y, 0), y_ref(y, 0), s_z.at[d], r_z.at[(4 - d) % 4], r, 4 * y + there
-                    )
-                )
-
-    def y_copies(k, act):
-        onward = need(across)
-
-        def one(way, to):
-            ref = y_ref(y, k)
-            act(remote(ref, ref, s_y.at[way, k], r_y.at[y, k], r, 4 * to + zh))
-
-        @pl.when(need(up) | onward if k % 2 == 0 else need(up))
-        def _():
-            one(0, up)
-
-        @pl.when(need(down) | onward if k % 2 == 1 else need(down))
-        def _():
-            one(1, down)
-
-    def relay(k, act):
-        owner, to = (down, up) if k % 2 == 0 else (up, down)
-        ref = y_ref(owner, k)
-
-        @pl.when(need(to))
-        def _():
-            act(remote(ref, ref, s_r.at[k], r_y.at[owner, k], r, 4 * to + zh))
-
-    def run_relay(k):
-        owner, to = (down, up) if k % 2 == 0 else (up, down)
-
-        @pl.when(need(y) | need(to))
-        def _():
-            arrived(y_ref(owner, k), r_y.at[owner, k])
-
-        relay(k, start)
-
-    @pl.when(r != c)
-    def _():
-        arrived(y_ref(y, 0), r_t.at[0])
-
-    @pl.when(r == c)
-    def _():
-        t_here.wait()
-
-    y_copies(0, start)
-    z_copies(start)
-
-    @pl.when(core == 1)
-    def _():
-        arrived(lead, r_sib.at[0])
-
-    lists = hall[pl.ds(pl.multiple_of(core * 8 * CAP, 8 * CAP), 8 * CAP)]
-    lout[...] = dot(lists, lead[...]).reshape(8, CAP, part)
-
-    def l_copies(act, act_here):
-        for j in range(8):
-            s = 2 * j + core
-            as_row = s >= c
-            row, col = jnp.where(as_row, s, c), jnp.where(as_row, c, s)
-            kind = jnp.where(as_row, 0, 1)
-            here = as_row & (s == r)
-
-            @pl.when(jnp.logical_not(here))
-            def _():
-                act(remote(lout.at[j], swaps.at[kind, q], s_l.at[j], r_l.at[kind, q], row, col))
-
-            @pl.when(here)
-            def _():
-                act_here(j)
-
-    def keep_lead(j):
-        swaps[0, q] = lout[j]
-
-    l_copies(start, keep_lead)
-
-    def run_y(k):
-        @pl.when(zh <= r)
-        def _():
-            arrived(y_ref(y, k), r_z.at[k])
-
-        y_copies(k, start)
+            hot = hall[128 * j : 128 * (j + 1)]
+            total = total + sum(dot16(term, hot) for term in split(listing, 3))
+        vbuf[core, q] = total
+        w_copies(start, vbuf, s_v, r_v)
 
     run_relay(0)
     run_y(1)
     run_y(3)
+
+    for d in range(1, 4):
+        p = lax.rem(pair + 2 * d, 8)
+
+        @pl.when(wanted(q))
+        def _():
+            arrived(qc.at[p, slot(core)], r_b.at[core, p])
+
+        forward(p)
+
+    @pl.when(c == 0)
+    def _():
+        for d in range(1, 8):
+            p = lax.rem(q + d, 8)
+            arrived(vbuf.at[core, p], r_v.at[p])
+        v_sib.start()
+        arrived(vbuf.at[1 - core], r_sib.at[3])
+        w0[...] = choose(hall_t[...], vbuf[...].reshape(16 * CAP, width))
+
+    @pl.when(c != 0)
+    def _():
+        arrived(corner, r_k.at[1])
+
+    @pl.when(r < c)
+    def _():
+        out[...] = jnp.zeros_like(out)
+
+    @pl.when(r >= c)
+    def _():
+        arrived(wbuf.at[1 - core], r_sib.at[2])
+        w1 = choose(hall_t[...], wbuf[...].reshape(16 * CAP, width))
+        for i, term in enumerate(split(w1, 3)):
+            w1s[i] = term
+        for p in range(8):
+            arrived(qc.at[p, slot(1 - core)], r_b.at[1 - core, p])
+        placed = [dot16(w1s[i], spread[...]) for i in range(2)]
+        hit = hit_col[...] > 0
+        for p in range(8):
+            cut = slice(p * part, (p + 1) * part)
+            value = qc[p]
+            if p < width // part:
+                value = jnp.where(c == 0, w0[:, cut], value)
+            for j, term in enumerate(split(value, 2)):
+                term = jnp.where(hit[:, cut], placed[j][:, cut], term.astype(F32))
+                panel[j, :, cut] = term.astype(BF16)
+        for p in range(8):
+            @pl.when(p != q)
+            def _():
+                arrived(swaps.at[0, p], r_l.at[0, p])
+        rows_in = jnp.concatenate([swaps[0, p] for p in range(8)], axis=1)
+        placed = sum(dot16(term, spread[...]) for term in split(corner[...], 3))
+        rows_in = jnp.where(hit, placed, rows_in)
+        for j, term in enumerate(split(rows_in, 3)):
+            right[j * CAP : (j + 1) * CAP] = term
+        col_piv = listed(place_row, piv_row[...], order(c) * CAP, CAP)
+        hot = hot16(one_hot(col_piv, col_start, (CAP, cols), 1))
+        for j in range(3):
+            right[(3 + j) * CAP : (4 + j) * CAP] = hot
+
     run_relay(1)
     run_relay(3)
     run_y(2)
 
-    @pl.when(wanted(6 + zl))
-    def _():
-        arrived(qc.at[pair, slot(core)], r_b.at[core, pair])
-
-    x_copies(start)
+    def tile_update(owner):
+        row_start = r * rows + owner * tile
+        hot = one_hot(left[...], row_start, (CAP, tile), 1).astype(F32)
+        hit = jnp.max(hot, axis=0, keepdims=True)
+        rows_t = jnp.concatenate([qr[2 * owner], qr[2 * owner + 1]], axis=1)
+        near = hot16(one_hot(piv_col[...], row_start, (width, tile), 1))
+        rows_t = jnp.where(hit > 0, sum(dot16(w1s[i], near) for i in range(3)), rows_t)
+        rows_t = jnp.where((r == 0) & (c == 0) & (owner == 0), w0[...], rows_t)
+        scaled = lax.dot_general(
+            coupling[...], rows_t, (((0,), (0,)), ((), ())),
+            precision=HIGHEST, preferred_element_type=F32,
+        )
+        s_hi, s_lo = split(scaled, 2)
+        lanes = ((0,), (0,))
+        change = dot16(s_hi, panel[0], lanes) + dot16(s_hi, panel[1], lanes)
+        change = change + dot16(s_lo, panel[0], lanes)
+        kind = jnp.where(r == c, 0, 1)
+        cols_in = jnp.concatenate([swaps[kind, 2 * owner + i] for i in range(2)], axis=1)
+        cols_in = jnp.where(hit > 0, 0.0, cols_in)
+        hot = hot.astype(BF16)
+        lhs = jnp.concatenate([hot, hot, hot] + split(cols_in, 3), axis=0)
+        moved = dot16(lhs, right[...], lanes)
+        at = pl.ds(pl.multiple_of(owner * tile, tile), tile)
+        gone = (column(hit) > 0) | (hit_col[...] > 0)
+        value = jnp.where(gone, 0.0, block[at]) + moved
+        places_col = lax.broadcasted_iota(jnp.int32, (tile, cols), 1) + col_start
+        below = lax.broadcasted_iota(jnp.int32, (tile, cols), 0) + row_start >= places_col
+        out[at] = jnp.where(below, value - change, 0.0)
+
+        @pl.when(c == 0)
+        def _():
+            out[at, :width] = jnp.where(below[:, :width], rows_t.T - change[:, :width], 0.0)
+
+    @pl.when(r > c)
+    def _():
+        for p in range(8):
+            arrived(swaps.at[1, p], r_l.at[1, p])
+
+    @pl.when(r >= c)
+    def _():
+        tile_update(y)
+
     run_relay(2)
 
     @pl.when(r >= c)
     def _():
-        for p in range(8):
-            @pl.when(p != q)
-            def _():
-                arrived(swaps.at[0, p], r_l.at[0, p])
-
-    @pl.when(c == 0)
-    def _():
-        for p in range(width // part):
-            corner[:, p * part : (p + 1) * part] = swaps[0, p]
-        k_copies(1, start)
-
-    @pl.when(wanted(q))
-    def _():
-        for d in range(1, 8):
-            p = lax.rem(q + d, 8)
-            arrived(wbuf.at[core, p], r_w.at[p])
-
-    w_sib = remote(wbuf.at[core], wbuf.at[core], s_sib.at[2], r_sib.at[2], sib, c)
-
-    @pl.when(sib >= c)
-    def _():
-        w_sib.start()
-
-    for d in range(1, 8):
-        p = lax.rem(q + d, 8)
-
-        @pl.when(wanted(q) & (p != pair))
-        def _():
-            arrived(qc.at[p, slot(core)], r_b.at[core, p])
-
-        @pl.when(sib >= c)
-        def _():
-            f_copy(d).start()
-
-    @pl.when(r >= c)
-    def _():
-        arrived(wbuf.at[1 - core], r_sib.at[2])
-        w1[...] = dot(hall[...], wbuf[...].reshape(16 * CAP, width), ((0,), (0,)))
-
-    @pl.when(r >= c)
-    def _():
-        for p in range(8):
-            arrived(qc.at[p, slot(1 - core)], r_b.at[1 - core, p])
         for k in range(4):
             owner = up if k % 2 == 0 else down
             arrived(y_ref(owner, k), r_y.at[owner, k])
+
+        def side(i, _):
+            tile_update(jnp.where(i == 0, up, down))
+            return 0
+
+        lax.fori_loop(0, 2, side, 0)
+        for k in range(4):
             arrived(y_ref(across, k), r_y.at[across, k])
-
-    @pl.when(r > c)
-    def _():
-        for p in range(8):
-            arrived(swaps.at[1, p], r_l.at[1, p])
+        tile_update(across)
 
     @pl.when(c != 0)
     def _():
-        arrived(corner, r_k.at[1])
         w0_copy(c).wait_send()
-
-    keep.wait()
 
     @pl.when(r == 0)
     def _():
@@ -923,12 +1025,18 @@
 
     a_sib.wait_send()
     for d in range(1, 8):
-        a_copy(d)[1].wait_send()
+        a_copy(d).wait_send()
 
     @pl.when(c == 0)
     def _():
         k_copies(0, sent)
         k_copies(1, sent)
+        w_copies(sent, vbuf, s_v, r_v)
+        v_sib.wait_send()
+
+        @pl.when(r == 0)
+        def _():
+            w2_copies(sent)
 
     @pl.when(r != c)
     def _():
@@ -936,7 +1044,7 @@
 
     b_copies(sent)
     x_copies(sent)
-    w_copies(sent)
+    w_copies(sent, wbuf, s_w, r_w)
     z_copies(sent)
     l_copies(sent, lambda j: None)
     for k in range(4):
@@ -946,188 +1054,59 @@
     @pl.when(sib >= c)
     def _():
         w_sib.wait_send()
-        for d in range(8):
-            f_copy(d).wait_send()
-
-
-def compact_exchange(matrix, piv_row):
+        for p in range(8):
+            f_copy(p).wait_send()
+
+
+def compact(matrix, piv_row, coupling):
     rows, cols = matrix.shape
     width = piv_row.shape[1]
     half, part = width // 2, cols // 8
     dma = pltpu.SemaphoreType.DMA
-    any_spec = pl.BlockSpec(memory_space=pl.ANY)
     vmem = pl.BlockSpec(memory_space=pltpu.VMEM)
-    panel = jax.ShapeDtypeStruct((8, width, part), F32)
     return pl.pallas_call(
         compact_kernel,
-        out_shape=(
-            panel,
-            panel,
-            jax.ShapeDtypeStruct((2, 8, CAP, part), F32),
-            jax.ShapeDtypeStruct((CAP, width), F32),
-            jax.ShapeDtypeStruct((width, width), F32),
-        ),
-        in_specs=[any_spec, vmem],
-        out_specs=(any_spec, any_spec, vmem, vmem, vmem),
+        out_shape=jax.ShapeDtypeStruct((rows, cols), F32),
+        in_specs=[pl.BlockSpec(memory_space=pl.ANY), vmem, vmem],
+        out_specs=vmem,
         scratch_shapes=[
             pltpu.VMEM((rows, cols), F32),
             pltpu.VMEM((CAP, cols), F32),
-            pltpu.VMEM((16 * CAP, width), F32),
+            pltpu.VMEM((16 * CAP, width), BF16),
+            pltpu.VMEM((width, 16 * CAP), BF16),
+            pltpu.VMEM((width, 1), jnp.int32),
+            pltpu.VMEM((width, cols), BF16),
+            pltpu.VMEM((1, cols), F32),
             pltpu.VMEM((2, 8, CAP, part), F32),
             pltpu.VMEM((width, part), F32),
             pltpu.VMEM((half, part), F32),
             pltpu.VMEM((2, 8, CAP, width), F32),
+            pltpu.VMEM((2, 8, CAP, width), F32),
             pltpu.VMEM((CAP, 128), F32),
             pltpu.VMEM((16, CAP, 128), F32),
+            pltpu.VMEM((16, CAP, width), F32),
+            pltpu.VMEM((CAP, width), F32),
             pltpu.VMEM((8, CAP, part), F32),
-            dma((8,)), dma((8,)), dma((3,)), dma((3,)), dma((8,)), dma((1,)),
-            dma((2, 16)), dma((2,)), dma((1,)), dma((16,)), dma((8,)), dma((8,)), dma((8,)), dma((2, 8)),
-            dma((4,)), dma((4,)), dma((2, 8)), dma((8,)), dma((1,)), dma((1,)), dma((4,)), dma((4,)),
-            dma((2, 4)), dma((4,)), dma((4, 4)),
-            dma((3,)),
-        ],
-        compiler_params=pltpu.CompilerParams(
-            collective_id=1, has_side_effects=True, vmem_limit_bytes=32 * 1024 * 1024
-        ),
-        name="compact_exchange",
-    )(matrix, piv_row)
-
-
-def compact_update_kernel(
-    piv_row, m, qc, qr, swaps, corner, w1, coupling, result, panel, right, left, piv_col, w1s,
-    outs, sems,
-):
-    r, c = lax.axis_index("row"), lax.axis_index("col")
-    tile, cols = m.shape
-    rows = tile * pl.num_programs(0)
-    width = coupling.shape[0]
-    part = qc.shape[2]
-    step = pl.program_id(0)
-    row_start = r * rows + step * tile
-    col_start = c * cols
-
-    def dot(a, b, dims=((0,), (0,))):
-        return lax.dot_general(a, b, (dims, ((), ())), preferred_element_type=F32)
-
-    across = ((1,), (0,))
-    slot = lax.rem(step, 2)
-    out = outs.at[slot]
-
-    def put(i):
-        at = pl.ds(pl.multiple_of(i * tile, tile), tile)
-        return pltpu.make_async_copy(outs.at[lax.rem(i, 2)], result.at[at], sems.at[lax.rem(i, 2)])
-
-    @pl.when(step >= 2)
-    def _():
-        put(step - 2).wait()
-
-    @pl.when(r < c)
-    def _():
-        out[...] = jnp.zeros_like(out)
-
-    @pl.when((r >= c) & (step == 0))
-    def _():
-        place_row = places(piv_row[...], rows)
-        piv_col[...] = column(piv_row[...])
-        spread = one_hot(piv_col[...], col_start, (width, cols), 1).astype(F32)
-        hit = jnp.max(spread, axis=0, keepdims=True) > 0
-        spread = spread.astype(BF16)
-        for i, term in enumerate(split(w1[...], 3)):
-            w1s[i] = term
-        placed = [dot(w1s[i], spread, across) for i in range(2)]
-        for i in range(8):
-            cut = slice(i * part, (i + 1) * part)
-            for j, term in enumerate(split(qc[i], 2)):
-                term = jnp.where(hit[:, cut], placed[j][:, cut], term.astype(F32))
-                panel[j, :, cut] = term.astype(BF16)
-        lead = jnp.concatenate([swaps[0, i] for i in range(8)], axis=1)
-        placed = sum(dot(term, spread, across) for term in split(corner[...], 3))
-        lead = jnp.where(hit, placed, lead)
-        for j, term in enumerate(split(lead, 3)):
-            right[j * CAP : (j + 1) * CAP] = term
-        col_piv = listed(place_row, piv_row[...], order(c) * CAP, CAP)
-        hot = one_hot(col_piv, col_start, (CAP, cols), 1).astype(F32).astype(BF16)
-        for j in range(3):
-            right[(3 + j) * CAP : (4 + j) * CAP] = hot
-        left[...] = listed(place_row, piv_row[...], order(r) * CAP, CAP)
-
-    @pl.when(r >= c)
-    def _():
-        hot = one_hot(left[...], row_start, (CAP, tile), 1).astype(F32)
-        hit = jnp.max(hot, axis=0, keepdims=True)
-        rows_t = jnp.concatenate([qr[0], qr[1]], axis=1)
-        spread = one_hot(piv_col[...], row_start, (width, tile), 1).astype(F32).astype(BF16)
-        placed = sum(dot(w1s[i], spread, across) for i in range(3))
-        rows_t = jnp.where(hit > 0, placed, rows_t)
-        scaled = lax.dot_general(
-            coupling[...], rows_t, (((0,), (0,)), ((), ())),
-            precision=HIGHEST, preferred_element_type=F32,
-        )
-        s_hi, s_lo = split(scaled, 2)
-        change = dot(s_hi, panel[0]) + dot(s_hi, panel[1]) + dot(s_lo, panel[0])
-        which = jnp.where(r == c, 0, 1)
-        lead = jnp.concatenate([swaps[which, 2 * step + i] for i in range(2)], axis=1)
-        lead = jnp.where(hit > 0, 0.0, lead)
-        hot = hot.astype(BF16)
-        lhs = jnp.concatenate([hot, hot, hot] + split(lead, 3), axis=0)
-        moved = dot(lhs, right[...])
-        hit_row = column(hit) > 0
-        hit_col = jnp.max(right[3 * CAP : 4 * CAP].astype(F32), axis=0, keepdims=True) > 0
-        value = jnp.where(hit_row | hit_col, 0.0, m[...]) + moved
-        places_col = lax.broadcasted_iota(jnp.int32, (tile, cols), 1) + col_start
-        below = lax.broadcasted_iota(jnp.int32, (tile, cols), 0) + row_start >= places_col
-        out[...] = jnp.where(below, value - change, 0.0)
-
-        @pl.when(c == 0)
-        def _():
-            out[:, :width] = jnp.where(
-                below[:, :width], rows_t.T - change[:, :width], 0.0
-            )
-
-    put(step).start()
-
-    @pl.when(step == pl.num_programs(0) - 1)
-    def _():
-        put(step - 1).wait()
-        put(step).wait()
-
-
-def compact_update(piv_row, matrix, qc, qr, swaps, corner, w1, coupling):
-    rows, cols = matrix.shape
-    width = coupling.shape[0]
-    part = cols // 8
-    tile = 2 * part
-
-    def whole(shape):
-        return pl.BlockSpec(shape, lambda i: (0,) * len(shape))
-
-    return pl.pallas_call(
-        compact_update_kernel,
-        grid=(rows // tile,),
-        out_shape=jax.ShapeDtypeStruct((rows, cols), F32),
-        in_specs=[
-            whole((1, width)),
-            pl.BlockSpec((tile, cols), lambda i: (i, 0)),
-            whole((8, width, part)),
-            pl.BlockSpec((2, width, part), lambda i: (i, 0, 0)),
-            whole((2, 8, CAP, part)),
-            whole((CAP, width)),
-            whole((width, width)),
-            whole((width, width)),
-        ],
-        out_specs=pl.BlockSpec(memory_space=pltpu.HBM),
-        scratch_shapes=[
+            pltpu.VMEM((2, 8, CAP, part), F32),
+            pltpu.VMEM((8, width, part), F32),
+            pltpu.VMEM((8, width, part), F32),
+            pltpu.VMEM((3, width, width), BF16),
+            pltpu.VMEM((width, width), F32),
             pltpu.VMEM((2, width, cols), BF16),
             pltpu.VMEM((6 * CAP, cols), BF16),
             pltpu.VMEM((CAP, 1), jnp.int32),
-            pltpu.VMEM((width, 1), jnp.int32),
-            pltpu.VMEM((3, width, width), BF16),
-            pltpu.VMEM((2, tile, cols), F32),
-            pltpu.SemaphoreType.DMA((2,)),
+            dma((8,)), dma((8,)), dma((4,)), dma((4,)), dma((8,)), dma((1,)),
+            dma((2, 16)), dma((2,)), dma((1,)), dma((16,)), dma((16,)), dma((1,)),
+            dma((8,)), dma((8,)), dma((8,)), dma((8,)), dma((8,)), dma((2, 8)),
+            dma((4,)), dma((4,)), dma((2, 8)), dma((8,)), dma((1,)), dma((1,)), dma((4,)), dma((4,)),
+            dma((2, 4)), dma((4,)), dma((4, 4)),
+            dma((1,)),
         ],
-        compiler_params=pltpu.CompilerParams(vmem_limit_bytes=32 * 1024 * 1024),
-        name="compact_update",
-    )(piv_row, matrix, qc, qr, swaps, corner, w1, coupling)
+        compiler_params=pltpu.CompilerParams(
+            collective_id=1, has_side_effects=True, vmem_limit_bytes=40 * 1024 * 1024
+        ),
+        name="compact",
+    )(matrix, piv_row, coupling)
 
 
 def per_device(matrix, pivots, coupling):
@@ -1135,9 +1114,8 @@
     rows = matrix.shape[0]
     piv_row = pivots.reshape(1, width)
 
-    def compact(matrix, pivots, coupling):
-        parts = compact_exchange(matrix, piv_row)
-        return compact_update(piv_row, matrix, *parts, coupling)
+    def few(matrix, pivots, coupling):
+        return compact(matrix, piv_row, coupling)
 
     def general(matrix, pivots, coupling):
         piv_col = pivots.reshape(width, 1)
@@ -1147,7 +1125,7 @@
 
     blocks = jnp.arange(16, dtype=jnp.int32)[:, None]
     counts = jnp.sum((piv_row // rows == blocks).astype(jnp.int32), axis=1)
-    return lax.cond(jnp.max(counts) <= CAP, compact, general, matrix, pivots, coupling)
+    return lax.cond(jnp.max(counts) <= CAP, few, general, matrix, pivots, coupling)
 
 
 def solution(mesh):

time: 63.3 us -> 73.6 us (1.16)
  the two profiles are of different devices: /device:TPU:1 before, /device:TPU:31 now
where the time goes in v4:
time: 73.6 us; the launch traced here: 73.5 us
  Pallas kernels  69.1 us (94%)
  local copies, waits for them, and re-layouts  2.02 us (3%)
  other arithmetic  1.44 us (2%)
    pallas_call x1, Pallas kernels, compact(): pl.pallas_call(compact_kernel, out_shape=jax.ShapeDtypeStruct((rows, cols...  69.1 us
    unnamed x1, local copies, waits for them, and re-layouts  2.02 us

profile of v4, /device:TPU:31, one launch (start us, length us, event | category | flops | bytes accessed | tf_op | source)
XLA Modules:
  0.0 73.5 jit_solution(14040999546226989923)
XLA Ops:
  0.0 0.7 and_select_fusion
  0.7 0.1 convert_reduce_fusion
  0.8 0.6 reduce_max.9
  2.1 69.4 %conditional.1 = (f32[1024,1024]{1,0:T(8,128)S(1)}) conditional(s32[]{:T(128)} %convert_element_type.7, (s32[256]{0:T(256)}, f32[1024,1024]{1,0:T(8,128)}, s32[1,256]{1,0:T(1,128)}, f32[256,256]{1,0:T(8,128)}) %tuple.17, (f32[1024,1024]{1,0:T(8,128)}, s32[1,256]{1,0:T(1,128)}, f32[256,256]{1,0:T(8,128)}) %tuple.18), branch_computations={%region_2.3_spmd, %region_3.4_spmd} | conditional | bytes 22026360 | solution.py:1128
  2.1 69.1 %compact.1 = f32[1024,1024]{1,0:T(8,128)S(1)} custom-call(f32[1024,1024]{1,0:T(8,128)} %get-tuple-element.28.matrix, s32[1,256]{1,0:T(1,128)} %get-tuple-element.29.piv_row, f32[256,256]{1,0:T(8,128)} %get-tuple-element.30.coupling), custom_call_target="tpu_custom_call" | custom-call | tf_op jit(solution)/shard_map/cond/branch_1_fun/compact/pallas_call | solution.py:1067
  71.5 2.0 %copy.13 = f32[1024,1024]{1,0:T(8,128)} copy(f32[1024,1024]{1,0:T(8,128)S(1)} %get-tuple-element.31) | data formatting | bytes 8388608

commit v5 on v4

--- a/solution.py
+++ b/solution.py
@@ -500,7 +500,7 @@
 def compact_kernel(
     matrix, piv_row, coupling, out,
     block, picked, hall, hall_t, piv_col, spread, hit_col,
-    abuf, lead, piece, wbuf, vbuf, w0out, w0in, w2out, corner, lout, swaps, qc, qr,
+    abuf, lead, piece, wbuf, vbuf, w0out, w0z, w0y, w2out, corner, lout, swaps, qc, qr,
     w1s, w0, panel, right, left,
     s_a, r_a, s_sib, r_sib, s_ld, r_ld, s_k, r_k, s_w0, r_w0, s_w2, r_w2, s_w, r_w, s_v, r_v,
     s_l, r_l, s_b, s_x, r_b, s_f, s_t, r_t, s_z, r_z, s_y, s_r, r_y, local,
@@ -541,7 +541,7 @@
     def signal(row, col):
         pl.semaphore_signal(barrier, inc=1, device_id=(row, col), device_id_type=MESH)
 
-    for d in (1, 3):
+    for d in (1, 2, 3):
         signal(r, lax.rem(y + d, 4) * 4 + zh)
     for d in (1, 2, 3):
         signal(r, 4 * y + lax.rem(zh + d, 4))
@@ -550,15 +550,6 @@
     def _():
         signal(c, r)
 
-    @pl.when(c != 0)
-    def _():
-        signal(r, 0)
-
-    @pl.when(c == 0)
-    def _():
-        for b in range(1, 16):
-            signal(r, b)
-
     @pl.when(r > c)
     def _():
         for j in range(8):
@@ -567,7 +558,7 @@
     for d in range(1, 16):
         signal(lax.rem(r + d, 16), c)
 
-    greeted = 15 + 2 + 3 + jnp.where(r == c, 0, 1) + jnp.where(c == 0, 15, 1)
+    greeted = 15 + 3 + 3 + jnp.where(r == c, 0, 1)
     greeted = greeted + lax.div(c - core + 1, 2)
 
     place_row = places(piv_row[...], rows)
@@ -598,17 +589,16 @@
     for d in range(1, 8):
         a_copy(d).start()
 
-    def k_copy(i, b):
+    def k_copies(i, act, along):
         src = wbuf.at[core, q] if i == 0 else corner
-        return remote(src, src, s_k.at[i, b], r_k.at[i], r, b)
-
-    def k_copies(i, act):
-        for b in range(1, 16):
-            act(k_copy(i, b))
-
-    @pl.when(c == 0)
-    def _():
-        k_copies(0, start)
+
+        @pl.when((c == 0) if along == 0 else (zh == 0))
+        def _():
+            for d in (1, 2, 3):
+                col = 4 * d if along == 0 else 4 * y + d
+                act(remote(src, src, s_k.at[i, 3 * along + d - 1], r_k.at[i], r, col))
+
+    k_copies(0, start, 0)
 
     def lead_copy(p):
         return remote(
@@ -633,16 +623,16 @@
         w2_copies(start)
         corner[...] = w2out[0]
 
-    def w0_copy(b):
-        return remote(w0out, w0in.at[b], s_w0.at[0], r_w0.at[b], r, 0)
+    w0_copy = remote(w0out, w0z.at[zh], s_w0.at[0], r_w0.at[0, zh], r, 4 * y)
+    w0_pair = remote(w0z.at[pl.ds(0, 2)], w0y.at[y], s_w0.at[1], r_w0.at[1, y], r, 0)
 
     here_piv = listed(place_row, piv_row[...], chunk * 128, 128)
     near = hot16(one_hot(here_piv, col_start, (128, cols), 1))
     w0out[...] = sum(dot16(term, near, ((1,), (1,))) for term in split(picked[...], 3))
 
-    @pl.when(c != 0)
-    def _():
-        w0_copy(c).start()
+    @pl.when(zh != 0)
+    def _():
+        w0_copy.start()
 
     for d in range(1, 8):
         p = lax.rem(q + d, 8)
@@ -719,6 +709,7 @@
     def _():
         arrived(wbuf.at[core, q], r_k.at[0])
 
+    k_copies(0, start, 1)
     w_copies(start, wbuf, s_w, r_w)
 
     lead_sib = remote(lead, lead, s_sib.at[0], r_sib.at[0], sib, c)
@@ -763,14 +754,6 @@
 
     l_copies(start, keep_lead)
 
-    @pl.when(c == 0)
-    def _():
-        @pl.when(r != 0)
-        def _():
-            arrived(corner, r_w2.at[0])
-
-        k_copies(1, start)
-
     hot = one_hot(piv_col[...], col_start, (width, cols), 1).astype(F32)
     hit_col[...] = jnp.max(hot, axis=0, keepdims=True)
     spread[...] = hot.astype(BF16)
@@ -842,6 +825,23 @@
     y_copies(0, start)
     z_copies(start)
 
+    @pl.when((c == 0) & (r != 0))
+    def _():
+        arrived(corner, r_w2.at[0])
+
+    k_copies(1, start, 0)
+
+    @pl.when(zh == 0)
+    def _():
+        for d in (1, 2, 3):
+            arrived(w0z.at[d], r_w0.at[0, d])
+        w0z[0] = w0out[...] + w0z[2]
+        w0z[1] = w0z[1] + w0z[3]
+
+        @pl.when(y != 0)
+        def _():
+            w0_pair.start()
+
     @pl.when(wanted(6 + zl))
     def _():
         arrived(qc.at[pair, slot(core)], r_b.at[core, pair])
@@ -872,19 +872,22 @@
 
     @pl.when(c == 0)
     def _():
-        for b in range(1, 16):
-            arrived(w0in.at[b], r_w0.at[b])
-        w0in[0] = w0out[...]
+        for d in (1, 2, 3):
+            arrived(w0y.at[d], r_w0.at[1, d])
+        w0y[0] = w0z[:2]
         total = jnp.zeros((CAP, width), F32)
         for j in range(4):
-            listing = sum(
-                w0in[b] for b in range(16) if ((b % 2) * 8 + b // 2) // 4 == j
-            )
+            listing = w0y[2 * (j % 2), j // 2] + w0y[2 * (j % 2) + 1, j // 2]
             hot = hall[128 * j : 128 * (j + 1)]
             total = total + sum(dot16(term, hot) for term in split(listing, 3))
         vbuf[core, q] = total
         w_copies(start, vbuf, s_v, r_v)
 
+    @pl.when((zh == 0) & (y != 0))
+    def _():
+        arrived(corner, r_k.at[1])
+
+    k_copies(1, start, 1)
     run_relay(0)
     run_y(1)
     run_y(3)
@@ -907,7 +910,7 @@
         arrived(vbuf.at[1 - core], r_sib.at[3])
         w0[...] = choose(hall_t[...], vbuf[...].reshape(16 * CAP, width))
 
-    @pl.when(c != 0)
+    @pl.when(zh != 0)
     def _():
         arrived(corner, r_k.at[1])
 
@@ -1010,9 +1013,17 @@
             arrived(y_ref(across, k), r_y.at[across, k])
         tile_update(across)
 
-    @pl.when(c != 0)
-    def _():
-        w0_copy(c).wait_send()
+    @pl.when(zh != 0)
+    def _():
+        w0_copy.wait_send()
+
+    @pl.when((zh == 0) & (y != 0))
+    def _():
+        w0_pair.wait_send()
+
+    for i in range(2):
+        for along in range(2):
+            k_copies(i, sent, along)
 
     @pl.when(r == 0)
     def _():
@@ -1029,8 +1040,6 @@
 
     @pl.when(c == 0)
     def _():
-        k_copies(0, sent)
-        k_copies(1, sent)
         w_copies(sent, vbuf, s_v, r_v)
         v_sib.wait_send()
 
@@ -1083,7 +1092,8 @@
             pltpu.VMEM((2, 8, CAP, width), F32),
             pltpu.VMEM((2, 8, CAP, width), F32),
             pltpu.VMEM((CAP, 128), F32),
-            pltpu.VMEM((16, CAP, 128), F32),
+            pltpu.VMEM((4, CAP, 128), F32),
+            pltpu.VMEM((4, 2, CAP, 128), F32),
             pltpu.VMEM((16, CAP, width), F32),
             pltpu.VMEM((CAP, width), F32),
             pltpu.VMEM((8, CAP, part), F32),
@@ -1096,7 +1106,7 @@
             pltpu.VMEM((6 * CAP, cols), BF16),
             pltpu.VMEM((CAP, 1), jnp.int32),
             dma((8,)), dma((8,)), dma((4,)), dma((4,)), dma((8,)), dma((1,)),
-            dma((2, 16)), dma((2,)), dma((1,)), dma((16,)), dma((16,)), dma((1,)),
+            dma((2, 6)), dma((2,)), dma((2,)), dma((2, 4)), dma((16,)), dma((1,)),
             dma((8,)), dma((8,)), dma((8,)), dma((8,)), dma((8,)), dma((2, 8)),
             dma((4,)), dma((4,)), dma((2, 8)), dma((8,)), dma((1,)), dma((1,)), dma((4,)), dma((4,)),
             dma((2, 4)), dma((4,)), dma((4, 4)),

time: 73.6 us -> 59.2 us (0.80)
  the two profiles are of different devices: /device:TPU:31 before, /device:TPU:1 now
where the time goes in v5:
time: 59.2 us; the launch traced here: 58.7 us
  Pallas kernels  54.3 us (92%)
  local copies, waits for them, and re-layouts  2.02 us (3%)
  other arithmetic  1.44 us (2%)
  between operations  0.66 us (1%)
    pallas_call x1, Pallas kernels, compact(): pl.pallas_call(compact_kernel, out_shape=jax.ShapeDtypeStruct((rows, cols...  54.3 us
    unnamed x1, local copies, waits for them, and re-layouts  2.02 us

profile of v5, /device:TPU:1, one launch (start us, length us, event | category | flops | bytes accessed | tf_op | source)
XLA Modules:
  0.0 58.7 jit_solution(15439920082728279061)
XLA Ops:
  0.0 0.7 %and_select_fusion = s32[256]{0:T(256)S(1)} fusion(s32[256]{0:T(256)} %param.6), kind=kLoop, calls=%fused_computation.2 | loop fusion | flops 3840 | bytes 2048 | tf_op jit(solution)/shard_map/jit(floor_divide)/jit(_where)/select_n | solution.py:1137
  0.7 0.1 convert_reduce_fusion
  0.8 0.6 %reduce_max.9 = s32[]{:T(128)} reduce(s32[16]{0:T(128)S(1)} %convert_reduce_fusion, s32[]{:T(128)} %constant.19.clone.1), dimensions={0}, to_apply=%region_1.2 | reduce | flops 15 | bytes 72 | tf_op jit(solution)/shard_map/reduce_max | solution.py:1138
  2.1 54.6 %conditional.1 = (f32[1024,1024]{1,0:T(8,128)S(1)}) conditional(s32[]{:T(128)} %convert_element_type.7, (s32[256]{0:T(256)}, f32[1024,1024]{1,0:T(8,128)}, s32[1,256]{1,0:T(1,128)}, f32[256,256]{1,0:T(8,128)}) %tuple.17, (f32[1024,1024]{1,0:T(8,128)}, s32[1,256]{1,0:T(1,128)}, f32[256,256]{1,0:T(8,128)}) %tuple.18), branch_computations={%region_2.3_spmd, %region_3.4_spmd} | conditional | bytes 22026360 | solution.py:1138
  2.1 54.3 %compact.1 = f32[1024,1024]{1,0:T(8,128)S(1)} custom-call(f32[1024,1024]{1,0:T(8,128)} %get-tuple-element.28.matrix, s32[1,256]{1,0:T(1,128)} %get-tuple-element.29.piv_row, f32[256,256]{1,0:T(8,128)} %get-tuple-element.30.coupling), custom_call_target="tpu_custom_call" | custom-call | tf_op jit(solution)/shard_map/cond/branch_1_fun/compact/pallas_call | solution.py:1076
  56.7 2.0 %copy.13 = f32[1024,1024]{1,0:T(8,128)} copy(f32[1024,1024]{1,0:T(8,128)S(1)} %get-tuple-element.31) | data formatting | bytes 8388608

commit v6 on v5

--- a/solution.py
+++ b/solution.py
@@ -512,7 +512,7 @@
     tile = 2 * part
     q, core = lax.div(r, 2), lax.rem(r, 2)
     zl = lax.rem(q, 2)
-    y, zh = lax.div(c, 4), lax.rem(c, 4)
+    x, y, zh = lax.div(r, 4), lax.div(c, 4), lax.rem(c, 4)
     sib = r + 1 - 2 * core
     pair = q + 1 - 2 * zl
     chunk = lax.div(order(c), 4)
@@ -712,48 +712,6 @@
     k_copies(0, start, 1)
     w_copies(start, wbuf, s_w, r_w)
 
-    lead_sib = remote(lead, lead, s_sib.at[0], r_sib.at[0], sib, c)
-
-    @pl.when(r == 0)
-    def _():
-        lead[...] = block[:width, :part]
-
-    @pl.when((core == 0) & (r != 0))
-    def _():
-        arrived(lead, r_ld.at[0])
-
-    @pl.when(core == 0)
-    def _():
-        lead_sib.start()
-
-    @pl.when(core == 1)
-    def _():
-        arrived(lead, r_sib.at[0])
-
-    lists = hall[pl.ds(pl.multiple_of(core * 8 * CAP, 8 * CAP), 8 * CAP)]
-    lout[...] = choose(lists, lead[...]).reshape(8, CAP, part)
-
-    def l_copies(act, act_here):
-        for j in range(8):
-            s = 2 * j + core
-            as_row = s >= c
-            row, col = jnp.where(as_row, s, c), jnp.where(as_row, c, s)
-            kind = jnp.where(as_row, 0, 1)
-            here = as_row & (s == r)
-
-            @pl.when(jnp.logical_not(here))
-            def _():
-                act(remote(lout.at[j], swaps.at[kind, q], s_l.at[j], r_l.at[kind, q], row, col))
-
-            @pl.when(here)
-            def _():
-                act_here(j)
-
-    def keep_lead(j):
-        swaps[0, q] = lout[j]
-
-    l_copies(start, keep_lead)
-
     hot = one_hot(piv_col[...], col_start, (width, cols), 1).astype(F32)
     hit_col[...] = jnp.max(hot, axis=0, keepdims=True)
     spread[...] = hot.astype(BF16)
@@ -779,35 +737,31 @@
                     )
                 )
 
+    def relays(node, k, way):
+        off = lax.rem(node + 4 - x, 4)
+        return (off == 2) | ((off != 0) & (way == k % 2))
+
     def y_copies(k, act):
-        onward = need(across)
-
-        def one(way, to):
+        for way, to in ((0, up), (1, down)):
             ref = y_ref(y, k)
-            act(remote(ref, ref, s_y.at[way, k], r_y.at[y, k], r, 4 * to + zh))
-
-        @pl.when(need(up) | onward if k % 2 == 0 else need(up))
-        def _():
-            one(0, up)
-
-        @pl.when(need(down) | onward if k % 2 == 1 else need(down))
-        def _():
-            one(1, down)
+
+            @pl.when(need(to) | (need(across) & relays(to, k, way)))
+            def _():
+                act(remote(ref, ref, s_y.at[way, k], r_y.at[y, k], r, 4 * to + zh))
 
     def relay(k, act):
-        owner, to = (down, up) if k % 2 == 0 else (up, down)
-        ref = y_ref(owner, k)
-
-        @pl.when(need(to))
-        def _():
-            act(remote(ref, ref, s_r.at[k], r_y.at[owner, k], r, 4 * to + zh))
+        for way, owner, to in ((0, down, up), (1, up, down)):
+            ref = y_ref(owner, k)
+
+            @pl.when(need(to) & relays(y, k, way))
+            def _():
+                act(remote(ref, ref, s_r.at[way, k], r_y.at[owner, k], r, 4 * to + zh))
 
     def run_relay(k):
-        owner, to = (down, up) if k % 2 == 0 else (up, down)
-
-        @pl.when(need(y) | need(to))
-        def _():
-            arrived(y_ref(owner, k), r_y.at[owner, k])
+        for way, owner, to in ((0, down, up), (1, up, down)):
+            @pl.when(relays(y, k, way) & (need(y) | need(to)))
+            def _():
+                arrived(y_ref(owner, k), r_y.at[owner, k])
 
         relay(k, start)
 
@@ -817,13 +771,6 @@
             arrived(y_ref(y, k), r_z.at[k])
 
         y_copies(k, start)
-
-    @pl.when(r != c)
-    def _():
-        arrived(y_ref(y, 0), r_t.at[0])
-
-    y_copies(0, start)
-    z_copies(start)
 
     @pl.when((c == 0) & (r != 0))
     def _():
@@ -842,33 +789,20 @@
         def _():
             w0_pair.start()
 
+    @pl.when(r != c)
+    def _():
+        arrived(y_ref(y, 0), r_t.at[0])
+
+    y_copies(0, start)
+    z_copies(start)
+
     @pl.when(wanted(6 + zl))
     def _():
         arrived(qc.at[pair, slot(core)], r_b.at[core, pair])
 
     x_copies(start)
     forward(pair)
-    for d in range(1, 4):
-        p = lax.rem(q + 2 * d, 8)
-
-        @pl.when(wanted(q))
-        def _():
-            arrived(qc.at[p, slot(core)], r_b.at[core, p])
-
-        forward(p)
-
-    @pl.when(wanted(q))
-    def _():
-        for d in range(1, 8):
-            p = lax.rem(q + d, 8)
-            arrived(wbuf.at[core, p], r_w.at[p])
-
-    w_sib = remote(wbuf.at[core], wbuf.at[core], s_sib.at[2], r_sib.at[2], sib, c)
-    v_sib = remote(vbuf.at[core], vbuf.at[core], s_sib.at[3], r_sib.at[3], sib, c)
-
-    @pl.when(sib >= c)
-    def _():
-        w_sib.start()
+    run_relay(0)
 
     @pl.when(c == 0)
     def _():
@@ -883,14 +817,82 @@
         vbuf[core, q] = total
         w_copies(start, vbuf, s_v, r_v)
 
-    @pl.when((zh == 0) & (y != 0))
-    def _():
-        arrived(corner, r_k.at[1])
-
-    k_copies(1, start, 1)
-    run_relay(0)
     run_y(1)
     run_y(3)
+    lead_sib = remote(lead, lead, s_sib.at[0], r_sib.at[0], sib, c)
+
+    @pl.when(r == 0)
+    def _():
+        lead[...] = block[:width, :part]
+
+    @pl.when((core == 0) & (r != 0))
+    def _():
+        arrived(lead, r_ld.at[0])
+
+    @pl.when(core == 0)
+    def _():
+        lead_sib.start()
+
+    @pl.when(core == 1)
+    def _():
+        arrived(lead, r_sib.at[0])
+
+    lists = hall[pl.ds(pl.multiple_of(core * 8 * CAP, 8 * CAP), 8 * CAP)]
+    lout[...] = choose(lists, lead[...]).reshape(8, CAP, part)
+
+    def l_copies(act, act_here):
+        for d in range(8):
+            j = lax.rem(q + d, 8)
+            s = 2 * j + core
+            as_row = s >= c
+            row, col = jnp.where(as_row, s, c), jnp.where(as_row, c, s)
+            kind = jnp.where(as_row, 0, 1)
+            here = as_row & (s == r)
+
+            @pl.when(jnp.logical_not(here))
+            def _():
+                act(remote(lout.at[j], swaps.at[kind, q], s_l.at[j], r_l.at[kind, q], row, col))
+
+            @pl.when(here)
+            def _():
+                act_here(j)
+
+    def keep_lead(j):
+        swaps[0, q] = lout[j]
+
+    l_copies(start, keep_lead)
+
+
+    w_sib = remote(wbuf.at[core], wbuf.at[core], s_sib.at[2], r_sib.at[2], sib, c)
+    v_sib = remote(vbuf.at[core], vbuf.at[core], s_sib.at[3], r_sib.at[3], sib, c)
+
+    @pl.when((zh == 0) & (y != 0))
+    def _():
+        arrived(corner, r_k.at[1])
+
+    k_copies(1, start, 1)
+    for d in range(1, 4):
+        p = lax.rem(q + 2 * d, 8)
+
+        @pl.when(wanted(q))
+        def _():
+            arrived(qc.at[p, slot(core)], r_b.at[core, p])
+
+        forward(p)
+
+    @pl.when(wanted(q))
+    def _():
+        for d in range(1, 8):
+            p = lax.rem(q + d, 8)
+            arrived(wbuf.at[core, p], r_w.at[p])
+
+    @pl.when(sib >= c)
+    def _():
+        w_sib.start()
+
+    run_relay(1)
+    run_relay(3)
+    run_y(2)
 
     for d in range(1, 4):
         p = lax.rem(pair + 2 * d, 8)
@@ -950,9 +952,6 @@
         for j in range(3):
             right[(3 + j) * CAP : (4 + j) * CAP] = hot
 
-    run_relay(1)
-    run_relay(3)
-    run_y(2)
 
     def tile_update(owner):
         row_start = r * rows + owner * tile
@@ -1001,8 +1000,10 @@
     @pl.when(r >= c)
     def _():
         for k in range(4):
-            owner = up if k % 2 == 0 else down
-            arrived(y_ref(owner, k), r_y.at[owner, k])
+            for way, owner in ((0, down), (1, up)):
+                @pl.when(jnp.logical_not(relays(y, k, way)))
+                def _():
+                    arrived(y_ref(owner, k), r_y.at[owner, k])
 
         def side(i, _):
             tile_update(jnp.where(i == 0, up, down))
@@ -1109,7 +1110,7 @@
             dma((2, 6)), dma((2,)), dma((2,)), dma((2, 4)), dma((16,)), dma((1,)),
             dma((8,)), dma((8,)), dma((8,)), dma((8,)), dma((8,)), dma((2, 8)),
             dma((4,)), dma((4,)), dma((2, 8)), dma((8,)), dma((1,)), dma((1,)), dma((4,)), dma((4,)),
-            dma((2, 4)), dma((4,)), dma((4, 4)),
+            dma((2, 4)), dma((2, 4)), dma((4, 4)),
             dma((1,)),
         ],
         compiler_params=pltpu.CompilerParams(
@@ -1134,7 +1135,8 @@
         return update(piv_col, piv_row, matrix, qc, qr, coupling)
 
     blocks = jnp.arange(16, dtype=jnp.int32)[:, None]
-    counts = jnp.sum((piv_row // rows == blocks).astype(jnp.int32), axis=1)
+    block = jnp.right_shift(piv_row, rows.bit_length() - 1)
+    counts = jnp.sum((block == blocks).astype(jnp.int32), axis=1)
     return lax.cond(jnp.max(counts) <= CAP, few, general, matrix, pivots, coupling)
 
 

time: 59.2 us -> 55.7 us (0.941)
  Pallas kernels: 54.3 us -> 50.6 us
    pallas_call x1, Pallas kernels: 54.3 us -> 50.6 us  [compact(): pl.pallas_call(compact_kernel, out_shape=jax.ShapeDtypeStruct((rows, cols...]
    select_n x1 -> x0, other arithmetic: 0.69 us -> none  [per_device(): counts = jnp.sum((piv_row // rows == blocks).astype(jnp.int32), axis=1)]
    shift_right_arithmetic x0 -> x1, other arithmetic: none -> 0.68 us  [per_device(): block = jnp.right_shift(piv_row, rows.bit_length() - 1)]
where the time goes in v6:
time: 55.7 us; the launch traced here: 55 us
  Pallas kernels  50.6 us (91%)
  local copies, waits for them, and re-layouts  2.02 us (4%)
  other arithmetic  1.43 us (3%)
  between operations  0.66 us (1%)
    pallas_call x1, Pallas kernels, compact(): pl.pallas_call(compact_kernel, out_shape=jax.ShapeDtypeStruct((rows, cols...  50.6 us
    unnamed x1, local copies, waits for them, and re-layouts  2.02 us

profile of v6, /device:TPU:1, one launch (start us, length us, event | category | flops | bytes accessed | tf_op | source)
XLA Modules:
  0.0 55.0 jit_solution(13768832741741736728)
XLA Ops:
  0.0 0.7 %broadcast_shift-right-arithmetic_fusion = s32[256]{0:T(256)S(1)} fusion(s32[256]{0:T(256)} %param.6), kind=kLoop, calls=%fused_computation.2 | loop fusion | flops 256 | bytes 2048 | tf_op jit(solution)/shard_map/shift_right_arithmetic | solution.py:1138
  0.7 0.1 convert_reduce_fusion
  0.8 0.6 %reduce_max.9 = s32[]{:T(128)} reduce(s32[16]{0:T(128)S(1)} %convert_reduce_fusion, s32[]{:T(128)} %constant.2.clone.1), dimensions={0}, to_apply=%region_1.0 | reduce | flops 15 | bytes 72 | tf_op jit(solution)/shard_map/reduce_max | solution.py:1140
  2.1 50.9 %conditional.1 = (f32[1024,1024]{1,0:T(8,128)S(1)}) conditional(s32[]{:T(128)} %convert_element_type.7, (s32[256]{0:T(256)}, f32[1024,1024]{1,0:T(8,128)}, s32[1,256]{1,0:T(1,128)}, f32[256,256]{1,0:T(8,128)}) %tuple.17, (f32[1024,1024]{1,0:T(8,128)}, s32[1,256]{1,0:T(1,128)}, f32[256,256]{1,0:T(8,128)}) %tuple.18), branch_computations={%region_2.0_spmd, %region_3.0_spmd} | conditional | bytes 22026360 | solution.py:1140
  2.1 50.6 %compact.1 = f32[1024,1024]{1,0:T(8,128)S(1)} custom-call(f32[1024,1024]{1,0:T(8,128)} %get-tuple-element.28.matrix, s32[1,256]{1,0:T(1,128)} %get-tuple-element.29.piv_row, f32[256,256]{1,0:T(8,128)} %get-tuple-element.30.coupling), custom_call_target="tpu_custom_call" | custom-call | tf_op jit(solution)/shard_map/cond/branch_1_fun/compact/pallas_call | solution.py:1077
  53.0 2.0 %copy.13 = f32[1024,1024]{1,0:T(8,128)} copy(f32[1024,1024]{1,0:T(8,128)S(1)} %get-tuple-element.31) | data formatting | bytes 8388608

commit v7 on v6

--- a/solution.py
+++ b/solution.py
@@ -978,8 +978,8 @@
         at = pl.ds(pl.multiple_of(owner * tile, tile), tile)
         gone = (column(hit) > 0) | (hit_col[...] > 0)
         value = jnp.where(gone, 0.0, block[at]) + moved
-        places_col = lax.broadcasted_iota(jnp.int32, (tile, cols), 1) + col_start
-        below = lax.broadcasted_iota(jnp.int32, (tile, cols), 0) + row_start >= places_col
+        places_col = lax.broadcasted_iota(jnp.int32, (1, cols), 1) + col_start
+        below = lax.broadcasted_iota(jnp.int32, (tile, 1), 0) + row_start >= places_col
         out[at] = jnp.where(below, value - change, 0.0)
 
         @pl.when(c == 0)
@@ -1135,8 +1135,8 @@
         return update(piv_col, piv_row, matrix, qc, qr, coupling)
 
     blocks = jnp.arange(16, dtype=jnp.int32)[:, None]
-    block = jnp.right_shift(piv_row, rows.bit_length() - 1)
-    counts = jnp.sum((block == blocks).astype(jnp.int32), axis=1)
+    inside = (piv_row >= blocks * rows) & (piv_row < (blocks + 1) * rows)
+    counts = jnp.sum(inside.astype(jnp.int32), axis=1)
     return lax.cond(jnp.max(counts) <= CAP, few, general, matrix, pivots, coupling)
 
 

time: 55.7 us -> 55.8 us (level)
    reduce_sum x1, other arithmetic: 0.12 us -> 0.86 us  [per_device(): counts = jnp.sum(inside.astype(jnp.int32), axis=1)]
    shift_right_arithmetic x1 -> x0, other arithmetic: 0.68 us -> none  [per_device(): block = jnp.right_shift(piv_row, rows.bit_length() - 1)]
where the time goes in v7:
time: 55.8 us; the launch traced here: 55 us
  Pallas kernels  50.6 us (91%)
  local copies, waits for them, and re-layouts  2.02 us (4%)
  other arithmetic  1.5 us (3%)
  between operations  0.66 us (1%)
    pallas_call x1, Pallas kernels, compact(): pl.pallas_call(compact_kernel, out_shape=jax.ShapeDtypeStruct((rows, cols...  50.6 us
    unnamed x1, local copies, waits for them, and re-layouts  2.02 us

profile of v7, /device:TPU:1, one launch (start us, length us, event | category | flops | bytes accessed | tf_op | source)
XLA Modules:
  0.0 55.0 jit_solution(10024638473596921936)
XLA Ops:
  0.0 0.9 %convert_reduce_fusion = s32[16]{0:T(128)S(1)} fusion(s32[256]{0:T(256)} %param.6, s32[16]{0:T(128)S(1)} %get-tuple-element.32, s32[16]{0:T(128)S(1)} %get-tuple-element.33), kind=kLoop, calls=%fused_computation | loop fusion | flops 20464 | bytes 1216 | tf_op jit(solution)/shard_map/reduce_sum | solution.py:1139
  0.9 0.6 %reduce_max.9 = s32[]{:T(128)} reduce(s32[16]{0:T(128)S(1)} %convert_reduce_fusion, s32[]{:T(128)} %constant.3.clone.1), dimensions={0}, to_apply=%region_1.0 | reduce | flops 15 | bytes 72 | tf_op jit(solution)/shard_map/reduce_max | solution.py:1140
  2.2 50.9 %conditional.1 = (f32[1024,1024]{1,0:T(8,128)S(1)}) conditional(s32[]{:T(128)} %convert_element_type.7, (s32[256]{0:T(256)}, f32[1024,1024]{1,0:T(8,128)}, s32[1,256]{1,0:T(1,128)}, f32[256,256]{1,0:T(8,128)}) %tuple.18, (f32[1024,1024]{1,0:T(8,128)}, s32[1,256]{1,0:T(1,128)}, f32[256,256]{1,0:T(8,128)}) %tuple.19), branch_computations={%region_2.0_spmd, %region_3.0_spmd} | conditional | bytes 22026360 | solution.py:1140
  2.2 50.6 %compact.1 = f32[1024,1024]{1,0:T(8,128)S(1)} custom-call(f32[1024,1024]{1,0:T(8,128)} %get-tuple-element.28.matrix, s32[1,256]{1,0:T(1,128)} %get-tuple-element.29.piv_row, f32[256,256]{1,0:T(8,128)} %get-tuple-element.30.coupling), custom_call_target="tpu_custom_call" | custom-call | tf_op jit(solution)/shard_map/cond/branch_1_fun/compact/pallas_call | solution.py:1077
  53.0 2.0 %copy.13 = f32[1024,1024]{1,0:T(8,128)} copy(f32[1024,1024]{1,0:T(8,128)S(1)} %get-tuple-element.31) | data formatting | bytes 8388608
  (1 shorter events, 0.0 us)

commit v8 on v7

--- a/solution.py
+++ b/solution.py
@@ -710,7 +710,6 @@
         arrived(wbuf.at[core, q], r_k.at[0])
 
     k_copies(0, start, 1)
-    w_copies(start, wbuf, s_w, r_w)
 
     hot = one_hot(piv_col[...], col_start, (width, cols), 1).astype(F32)
     hit_col[...] = jnp.max(hot, axis=0, keepdims=True)
@@ -802,6 +801,7 @@
 
     x_copies(start)
     forward(pair)
+    w_copies(start, wbuf, s_w, r_w)
     run_relay(0)
 
     @pl.when(c == 0)

time: 55.8 us -> 58 us (1.039)
  Pallas kernels: 50.6 us -> 53.4 us
    pallas_call x1, Pallas kernels: 50.6 us -> 53.4 us  [compact(): pl.pallas_call(compact_kernel, out_shape=jax.ShapeDtypeStruct((rows, cols...]
where the time goes in v8:
time: 58 us; the launch traced here: 57.8 us
  Pallas kernels  53.4 us (92%)
  local copies, waits for them, and re-layouts  2.02 us (3%)
  other arithmetic  1.5 us (3%)
  between operations  0.66 us (1%)
    pallas_call x1, Pallas kernels, compact(): pl.pallas_call(compact_kernel, out_shape=jax.ShapeDtypeStruct((rows, cols...  53.4 us
    unnamed x1, local copies, waits for them, and re-layouts  2.02 us

profile of v8, /device:TPU:1, one launch (start us, length us, event | category | flops | bytes accessed | tf_op | source)
XLA Modules:
  0.0 57.8 jit_solution(6250621170477539041)
XLA Ops:
  0.0 0.9 %convert_reduce_fusion = s32[16]{0:T(128)S(1)} fusion(s32[256]{0:T(256)} %param.6, s32[16]{0:T(128)S(1)} %get-tuple-element.32, s32[16]{0:T(128)S(1)} %get-tuple-element.33), kind=kLoop, calls=%fused_computation | loop fusion | flops 20464 | bytes 1216 | tf_op jit(solution)/shard_map/reduce_sum | solution.py:1139
  0.9 0.6 %reduce_max.9 = s32[]{:T(128)} reduce(s32[16]{0:T(128)S(1)} %convert_reduce_fusion, s32[]{:T(128)} %constant.3.clone.1), dimensions={0}, to_apply=%region_1.0 | reduce | flops 15 | bytes 72 | tf_op jit(solution)/shard_map/reduce_max | solution.py:1140
  2.2 53.6 %conditional.1 = (f32[1024,1024]{1,0:T(8,128)S(1)}) conditional(s32[]{:T(128)} %convert_element_type.7, (s32[256]{0:T(256)}, f32[1024,1024]{1,0:T(8,128)}, s32[1,256]{1,0:T(1,128)}, f32[256,256]{1,0:T(8,128)}) %tuple.18, (f32[1024,1024]{1,0:T(8,128)}, s32[1,256]{1,0:T(1,128)}, f32[256,256]{1,0:T(8,128)}) %tuple.19), branch_computations={%region_2.0_spmd, %region_3.0_spmd} | conditional | bytes 22026360 | solution.py:1140
  2.2 53.4 %compact.1 = f32[1024,1024]{1,0:T(8,128)S(1)} custom-call(f32[1024,1024]{1,0:T(8,128)} %get-tuple-element.28.matrix, s32[1,256]{1,0:T(1,128)} %get-tuple-element.29.piv_row, f32[256,256]{1,0:T(8,128)} %get-tuple-element.30.coupling), custom_call_target="tpu_custom_call" | custom-call | tf_op jit(solution)/shard_map/cond/branch_1_fun/compact/pallas_call | solution.py:1077
  55.8 2.0 %copy.13 = f32[1024,1024]{1,0:T(8,128)} copy(f32[1024,1024]{1,0:T(8,128)S(1)} %get-tuple-element.31) | data formatting | bytes 8388608
  (1 shorter events, 0.0 us)
